TPU v7x, 128 devices: a whole 4x4x4 slice. The times are simulated.
128 devices in a mesh: dp: 8 (over x, core), tensor: 16 (over z, y).
Axes of the slice: x: 4, y: 4, z: 4, core: 2. Of those that a mesh axis runs over, the one named last changes fastest.
Arguments:
- tokens: bfloat16 [3072, 4096], P('dp', 'tensor'), may hold values from -6 to 6
- gate_weight_codes: bfloat16 [4096, 14336], P(None, 'tensor')
- up_weight_codes: bfloat16 [4096, 14336], P(None, 'tensor')
- down_weight_codes: bfloat16 [14336, 4096], P('tensor')
- gate_channel_scale: float32 [14336], P('tensor'), may hold values from 0.0001 to 0.0004
- up_channel_scale: float32 [14336], P('tensor'), may hold values from 0.0001 to 0.0004
- down_channel_scale: float32 [4096], P('tensor'), may hold values from 0.0001 to 0.0004
- adapter_input_factors: bfloat16 [4096, 1024], P(None, 'dp'), may hold values from -0.09375 to 0.09375
- adapter_output_factors: bfloat16 [14336, 1024], P('tensor', 'dp'), may hold values from -0.8984375 to 0.8984375
- group_adapter_lists: int32 [8, 8, 2], replicated, may hold values from -1 to 7, as said below
- row_adapter_entry: int32 [3072], P('dp'), may hold values from 0 to 15, as said below
Outputs:
- mixed: bfloat16 [3072, 4096], P('dp', 'tensor')
Inputs may be any that keep to these rules, and one draw needn't show every extreme that they name: `group_adapter_lists`: entry (g, o, s) is the index, among the 8 adapters that owner group o holds, of the s-th adapter that group g takes from o, or -1 for an unused slot. Filled slots of a pair come first and name different adapters. Every group has a filled slot, and in every draw some group fills all 2 slots from every owner. Row r of group g = r // 384 reads owner o = row_adapter_entry // 2 and slot s = row_adapter_entry % 2; group_adapter_lists[g, o, s] is always filled.
All inputs are finite; a program needn't handle non-finite values.
Results may differ from a plain program's by a relative error of at most 0.0059.
Values may be sent and summed in bfloat16 or wider, within the bound.
A program may use at most 128 MiB of HBM per device.

v0:
```python
import math

import jax
import jax.numpy as jnp
from jax import lax
from jax.sharding import PartitionSpec as P

HIDDEN_UNITS = 14336
ADAPTER_RANK = 16


def from_partner(x, axis, apart):
    return lax.ppermute(x, axis, [(i, i ^ 1 << apart) for i in range(lax.axis_size(axis))])


def sylvester_table(order):
    first = jnp.arange(order, dtype=jnp.int32)[:, None]
    second = jnp.arange(order, dtype=jnp.int32)[None, :]
    common = first & second
    parity = jnp.zeros((order, order), jnp.int32)
    for bit_number in range(max(order.bit_length() - 1, 0)):
        parity = parity + (common >> bit_number & 1)
    return (1 - 2 * (parity % 2)).astype(jnp.float32)


def paley_table():
    index = jnp.arange(28, dtype=jnp.int32)
    outer_index = index // 2
    inner_index = index % 2
    left = outer_index[:, None]
    right = outer_index[None, :]
    offset = (right - left) % 13
    square = (
        (offset == 1)
        | (offset == 3)
        | (offset == 4)
        | (offset == 9)
        | (offset == 10)
        | (offset == 12)
    )
    legendre = jnp.where(offset == 0, 0.0, jnp.where(square, 1.0, -1.0))
    edge = (left == 0) | (right == 0)
    corner = (left == 0) & (right == 0)
    conference = jnp.where(corner, 0.0, jnp.where(edge, 1.0, legendre)).astype(jnp.float32)
    low_row = inner_index[:, None]
    low_col = inner_index[None, :]
    first_block = jnp.where((low_row == 1) & (low_col == 1), -1.0, 1.0).astype(jnp.float32)
    second_block = jnp.where((low_row == 0) & (low_col == 0), 1.0, -1.0).astype(jnp.float32)
    diagonal = (left == right).astype(jnp.float32)
    return conference * first_block + diagonal * second_block


def local(
    tokens,
    gate_weight_codes,
    up_weight_codes,
    down_weight_codes,
    gate_channel_scale,
    up_channel_scale,
    down_channel_scale,
    adapter_input_factors,
    adapter_output_factors,
    group_adapter_lists,
    row_adapter_entry,
):
    local_units = gate_weight_codes.shape[1]
    my_group = lax.axis_index("dp")
    slot_count = group_adapter_lists.shape[2]
    group_adapters = adapter_input_factors.shape[1] // ADAPTER_RANK
    left_all, right_all = (
        lax.all_gather(adapter_input_factors, "dp", axis=1, tiled=True),
        lax.all_gather(adapter_output_factors, "dp", axis=1, tiled=True),
    )
    mine = lax.dynamic_index_in_dim(group_adapter_lists, my_group, 0, keepdims=False)
    block = row_adapter_entry // slot_count * group_adapters + mine.reshape(-1)[row_adapter_entry]
    factor_columns = left_all.shape[1]
    piece = lax.all_gather(tokens, "tensor", axis=1, tiled=True)
    gate_raw = jnp.dot(piece, gate_weight_codes, preferred_element_type=jnp.float32)
    up_raw = jnp.dot(piece, up_weight_codes, preferred_element_type=jnp.float32)
    low_rank_everyall = jnp.dot(piece, left_all, preferred_element_type=jnp.float32)
    column_block = jnp.arange(factor_columns) // ADAPTER_RANK
    keep = column_block[None, :] == block[:, None]
    low_rank_rows = jnp.where(keep, low_rank_everyall, jnp.zeros_like(low_rank_everyall)).astype(
        jnp.bfloat16
    )
    adapter_extra = lax.dot_general(
        low_rank_rows, right_all, (((1,), (1,)), ((), ())), preferred_element_type=jnp.float32
    )
    gate = gate_raw * gate_channel_scale
    up = up_raw * up_channel_scale + adapter_extra
    hidden = (jax.nn.silu(gate) * up).astype(jnp.bfloat16)
    device_count = lax.axis_size("tensor")
    norm_factor = 1.0 / math.sqrt(HIDDEN_UNITS)
    walsh_local = local_units // 28
    outer_table = sylvester_table(walsh_local)
    inner_table = paley_table()
    local_table = (
        (outer_table[:, None, :, None] * inner_table[None, :, None, :])
        .reshape(local_units, local_units)
        .astype(jnp.bfloat16)
    )
    spread = jnp.dot(hidden, local_table, preferred_element_type=jnp.float32) * norm_factor
    for bit_number in range(device_count.bit_length() - 1):
        partner = from_partner(spread, "tensor", bit_number)
        upper = lax.axis_index("tensor") >> bit_number & 1
        spread = jnp.where(upper == 1, partner - spread, spread + partner)
    rotated = spread.astype(jnp.bfloat16)
    summed = lax.psum_scatter(
        lax.dot_general(
            down_weight_codes, rotated, (((0,), (1,)), ((), ())), preferred_element_type=jnp.float32
        ),
        "tensor",
        scatter_dimension=0,
        tiled=True,
    )
    return (jnp.transpose(summed) * down_channel_scale).astype(jnp.bfloat16)


def solution(mesh):
    return jax.shard_map(
        local,
        mesh=mesh,
        in_specs=(
            P("dp", "tensor"),
            P(None, "tensor"),
            P(None, "tensor"),
            P("tensor", None),
            P("tensor"),
            P("tensor"),
            P("tensor"),
            P(None, "dp"),
            P("tensor", "dp"),
            P(),
            P("dp"),
        ),
        out_specs=P("dp", "tensor"),
        check_vma=False,
    )
```

profile of v0, /device:TPU:0, one launch (start us, length us, event | category | flops | bytes accessed | tf_op | source)
XLA Modules:
  0.0 384.9 jit_solution(681894868376939895)
XLA Ops:
  9.2 4.8 %multiply_convert_fusion = bf16[32,28,32,28]{3,2,1,0:T(8,128)(2,1)} fusion(f32[28,28]{1,0:T(8,128)S(1)} %select_add_fusion, f32[32,32]{1,0:T(8,128)S(1)} %fusion.8), kind=kLoop, calls=%fused_computation | loop fusion | flops 1605632 | bytes 1612864 | tf_op jit(solution)/shard_map/convert_element_type | solution.py:100
  13.9 13.6 %convert_element_type.33 = bf16[896,896]{1,0:T(8,128)(2,1)S(1)} reshape(bf16[32,28,32,28]{3,2,1,0:T(8,128)(2,1)} %multiply_convert_fusion) | data formatting | bytes 3211264 | tf_op jit(solution)/shard_map/convert_element_type | solution.py:100
  28.3 9.9 %fusion.29 = s32[384]{0:T(512)S(1)} fusion(s32[384]{0:T(512)S(1)} %copy-done.3, s32[]{:T(128)} %bitcast, s32[]{:T(128)} %bitcast.1, s32[]{:T(128)} %bitcast.2, s32[]{:T(128)} %bitcast.3, s32[]{:T(128)} %bitcast.4, s32[]{:T(128)} %bitcast.5, s32[]{:T(128)} %bitcast.6, s32[]{:T(128)} %bitcast.7, s32[]{:T(128)} %bitcast.8, s32[]{:T(128)} %bitcast.9, ...), kind=kLoop, calls=%fused_computation.56 | loop fusion | flops 18816 | bytes 3136 | tf_op jit(solution)/shard_map/add | solution.py:75
  38.2 26.6 %all-gather.4.cloned.1.call-done = bf16[384,4096]{1,0:T(8,128)(2,1)} async-done(((bf16[384,256]{1,0:T(8,128)(2,1)}), bf16[384,4096]{1,0:T(8,128)(2,1)}) %all-gather.4.cloned.1.call-update) | async-done | bytes 3145744 | tf_op jit(solution)/shard_map/all_gather | solution.py:77
  64.7 8.7 %convolution_multiply_fusion.1 = f32[384,896]{1,0:T(8,128)} fusion(bf16[384,4096]{1,0:T(8,128)(2,1)} %all-gather.4.cloned.1.call-done, bf16[4096,896]{1,0:T(8,128)(2,1)} %param.13, f32[896]{0:T(1024)S(1)} %copy-done.6), kind=kOutput, calls=%fused_computation.6 | convolution fusion | flops 2818916352 | bytes 11865600 | tf_op jit(solution)/shard_map/dot_general | solution.py:79
  73.4 7.2 %convolution_multiply_fusion.2 = f32[384,896]{1,0:T(8,128)} fusion(bf16[384,4096]{1,0:T(8,128)(2,1)S(1)} %copy-done.5, bf16[4096,896]{1,0:T(8,128)(2,1)} %param.12, f32[896]{0:T(1024)S(1)} %copy-done.7), kind=kOutput, calls=%fused_computation.7 | convolution fusion | flops 2818916352 | bytes 11865600 | tf_op jit(solution)/shard_map/dot_general | solution.py:78
  80.6 38.9 %all-gather.6.cloned.1.call-done = bf16[4096,1024]{1,0:T(8,128)(2,1)} async-done(((bf16[4096,128]{1,0:T(8,128)(2,1)}), bf16[4096,1024]{1,0:T(8,128)(2,1)}) %all-gather.6.cloned.1.call-update) | async-done | bytes 8388624 | tf_op jit(solution)/shard_map/all_gather | solution.py:71
  119.5 8.6 %select_convert_fusion = bf16[384,1024]{1,0:T(8,128)(2,1)} fusion(bf16[384,4096]{1,0:T(8,128)(2,1)} %all-gather.4.cloned.1.call-done, bf16[4096,1024]{1,0:T(8,128)(2,1)} %all-gather.6.cloned.1.call-done, s32[1024]{0:T(1024)S(1)} %add_select_fusion.5, s32[384]{0:T(512)S(1)} %fusion.29), kind=kOutput, calls=%fused_computation.2 | convolution fusion | flops 3222405120 | bytes 12326400 | tf_op jit(solution)/shard_map/dot_general | solution.py:80
  128.2 20.2 %all-gather.8.cloned.1.call-done = bf16[896,1024]{1,0:T(8,128)(2,1)} async-done(((bf16[896,128]{1,0:T(8,128)(2,1)}), bf16[896,1024]{1,0:T(8,128)(2,1)}) %all-gather.8.cloned.1.call-update) | async-done | bytes 1835024 | tf_op jit(solution)/shard_map/all_gather | solution.py:72
  148.4 4.5 %convolution_multiply_fusion = f32[384,896]{1,0:T(8,128)S(1)} fusion(bf16[896,896]{1,0:T(8,128)(2,1)S(1)} %convert_element_type.33, f32[384,896]{1,0:T(8,128)} %convolution_multiply_fusion.1, bf16[384,1024]{1,0:T(8,128)(2,1)} %select_convert_fusion, bf16[896,1024]{1,0:T(8,128)(2,1)} %all-gather.8.cloned.1.call-done, f32[384,896]{1,0:T(8,128)} %convolution_multiply_fusion.2), kind=kOutput, calls=%fused_computation.3 | convolution fusion | flops 1323958272 | bytes 8355840 | tf_op jit(solution)/shard_map/dot_general | solution.py:102
  152.9 1.6 collective-permute-start
  154.4 30.8 %collective-permute-done = f32[384,896]{1,0:T(8,128)S(1)} collective-permute-done((f32[384,896]{1,0:T(8,128)S(1)}, f32[384,896]{1,0:T(8,128)S(1)}, u32[]{:S(2)}, u32[]{:S(2)}) %collective-permute-start) | collective-permute-done | bytes 1376288 | tf_op jit(solution)/shard_map/ppermute | solution.py:13
  185.3 1.6 add_select_fusion.2
  186.9 3.3 collective-permute-start.1
  190.2 30.1 %collective-permute-done.1 = f32[384,896]{1,0:T(8,128)} collective-permute-done((f32[384,896]{1,0:T(8,128)S(1)}, f32[384,896]{1,0:T(8,128)}, u32[]{:S(2)}, u32[]{:S(2)}) %collective-permute-start.1) | collective-permute-done | bytes 1376288 | tf_op jit(solution)/shard_map/ppermute | solution.py:13
  220.3 1.6 add_select_fusion.1
  221.9 1.6 collective-permute-start.2
  223.5 29.1 %collective-permute-done.2 = f32[384,896]{1,0:T(8,128)} collective-permute-done((f32[384,896]{1,0:T(8,128)S(1)}, f32[384,896]{1,0:T(8,128)}, u32[]{:S(2)}, u32[]{:S(2)}) %collective-permute-start.2) | collective-permute-done | bytes 1376288 | tf_op jit(solution)/shard_map/ppermute | solution.py:13
  252.6 1.6 add_select_fusion
  254.2 3.2 collective-permute-start.3
  257.5 28.0 %collective-permute-done.3 = f32[384,896]{1,0:T(8,128)S(1)} collective-permute-done((f32[384,896]{1,0:T(8,128)S(1)}, f32[384,896]{1,0:T(8,128)S(1)}, u32[]{:S(2)}, u32[]{:S(2)}) %collective-permute-start.3) | collective-permute-done | bytes 1376288 | tf_op jit(solution)/shard_map/ppermute | solution.py:13
  285.5 8.4 %convolution_bitcast_fusion = f32[4096,384]{0,1:T(8,128)} fusion(bf16[896,4096]{1,0:T(8,128)(2,1)} %param.14, f32[384,896]{1,0:T(8,128)S(1)} %add_select_fusion, f32[384,896]{1,0:T(8,128)S(1)} %collective-permute-done.3, pred[]{:T(512)S(6)} %eq.156), kind=kOutput, calls=%fused_computation.1 | convolution fusion | flops 2819948544 | bytes 16384001 | tf_op jit(solution)/shard_map/dot_general | solution.py:109
  294.0 82.7 %reduce-scatter.2.cloned.1.call-done = f32[256,384]{0,1:T(8,128)} async-done(((f32[4096,384]{0,1:T(8,128)}), f32[256,384]{0,1:T(8,128)}) %reduce-scatter.2.cloned.1.call-update) | async-done | bytes 393232 | tf_op jit(solution)/shard_map/reduce_scatter | solution.py:108
  376.7 1.7 fusion.4
  (34 shorter events, 3.3 us)
Async XLA Ops:
  6.5 2.3 copy-start
  6.5 58.2 %all-gather.4.cloned.1.call-start = ((), (), s32[]{:S(2)}) async-start(), calls=%async_computation.1 | async-start | bytes 3342336 | tf_op jit(solution)/shard_map/all_gather | solution.py:77
  7.3 112.3 %all-gather.6.cloned.1.call-start = ((), (), s32[]{:S(2)}) async-start(), calls=%async_computation.2 | async-start | bytes 9437184 | tf_op jit(solution)/shard_map/all_gather | solution.py:71
  8.0 140.3 %all-gather.8.cloned.1.call-start = ((), (), s32[]{:S(2)}) async-start(), calls=%async_computation.3 | async-start | bytes 2064384 | tf_op jit(solution)/shard_map/all_gather | solution.py:72
  8.7 367.9 %reduce-scatter.2.cloned.1.call-start = ((), (), s32[]{:S(2)}) async-start(), calls=%async_computation.4 | async-start | bytes 6684672 | tf_op jit(solution)/shard_map/reduce_scatter | solution.py:108
  13.9 14.3 %copy-start.3 = (s32[384]{0:T(512)S(1)}, s32[384]{0:T(512)}, u32[]{:S(2)}) copy-start(s32[384]{0:T(512)} %param.21) | copy-start | bytes 4612
  13.9 50.8 %copy-start.6 = (f32[896]{0:T(1024)S(1)}, f32[896]{0:T(1024)}, u32[]{:S(2)}) copy-start(f32[896]{0:T(1024)} %param.16) | copy-start | bytes 10756
  38.1 35.3 %copy-start.7 = (f32[896]{0:T(1024)S(1)}, f32[896]{0:T(1024)}, u32[]{:S(2)}) copy-start(f32[896]{0:T(1024)} %param.15) | copy-start | bytes 10756
  64.7 8.7 %copy-start.5 = (bf16[384,4096]{1,0:T(8,128)(2,1)S(1)}, bf16[384,4096]{1,0:T(8,128)(2,1)}, u32[]{:S(2)}) copy-start(bf16[384,4096]{1,0:T(8,128)(2,1)} %all-gather.4.cloned.1.call-done) | copy-start | bytes 9437188
  152.9 1.6 copy-start.2
  152.9 32.4 %collective-permute-start = (f32[384,896]{1,0:T(8,128)S(1)}, f32[384,896]{1,0:T(8,128)S(1)}, u32[]{:S(2)}, u32[]{:S(2)}) collective-permute-start(f32[384,896]{1,0:T(8,128)S(1)} %convolution_multiply_fusion), channel_id=1, source_target_pairs={{0,1},{1,0},{2,3},{3,2},{4,5},{5,4},{6,7},{7,6},{8,9},{9,8},{10,11... | collective-permute-start | bytes 4128776 | tf_op jit(solution)/shard_map/ppermute | solution.py:13
  186.9 33.4 %collective-permute-start.1 = (f32[384,896]{1,0:T(8,128)S(1)}, f32[384,896]{1,0:T(8,128)}, u32[]{:S(2)}, u32[]{:S(2)}) collective-permute-start(f32[384,896]{1,0:T(8,128)S(1)} %add_select_fusion.2), channel_id=1, source_target_pairs={{0,2},{1,3},{2,0},{3,1},{4,6},{5,7},{6,4},{7,5},{8,10},{9,11},{10,... | collective-permute-start | bytes 4128776 | tf_op jit(solution)/shard_map/ppermute | solution.py:13
  221.9 30.8 %collective-permute-start.2 = (f32[384,896]{1,0:T(8,128)S(1)}, f32[384,896]{1,0:T(8,128)}, u32[]{:S(2)}, u32[]{:S(2)}) collective-permute-start(f32[384,896]{1,0:T(8,128)S(1)} %add_select_fusion.1), channel_id=1, source_target_pairs={{0,4},{1,5},{2,6},{3,7},{4,0},{5,1},{6,2},{7,3},{8,12},{9,13},{10,... | collective-permute-start | bytes 4128776 | tf_op jit(solution)/shard_map/ppermute | solution.py:13
  254.2 31.3 %collective-permute-start.3 = (f32[384,896]{1,0:T(8,128)S(1)}, f32[384,896]{1,0:T(8,128)S(1)}, u32[]{:S(2)}, u32[]{:S(2)}) collective-permute-start(f32[384,896]{1,0:T(8,128)S(1)} %add_select_fusion), channel_id=1, source_target_pairs={{0,8},{1,9},{2,10},{3,11},{4,12},{5,13},{6,14},{7,15},{8,0},{9,1},... | collective-permute-start | bytes 4128776 | tf_op jit(solution)/shard_map/ppermute | solution.py:13
  293.9 82.8 %copy-start.4 = (f32[256]{0:T(256)S(1)}, f32[256]{0:T(256)}, u32[]{:S(2)}) copy-start(f32[256]{0:T(256)} %param.17) | copy-start | bytes 3076
  293.9 84.4 %copy-start.1 = (s32[8,8,2]{1,2,0:T(2,128)S(1)}, s32[8,8,2]{1,2,0:T(2,128)}, u32[]{:S(2)}) copy-start(s32[8,8,2]{1,2,0:T(2,128)} %param.20) | copy-start | bytes 1540
Sparse Core Ops, SparseCore 0:
  9.5 55.1 all-gather.3
  66.4 53.1 all-gather.5
  121.2 27.0 all-gather.7
  294.1 82.5 reduce-scatter.1
where the time goes:
time: 385 us
  waiting for transfers between devices  289 us (75%)
  matrix products  37.5 us (10%)
  other arithmetic  21.3 us (6%)
  local copies, waits for them, and re-layouts  14.5 us (4%)
  between operations  13.3 us (3%)
  starting transfers between devices  9.83 us (3%)
    ppermute x4, waiting for transfers between devices, from_partner(): lax.ppermute(x, axis, [(i, i ^ 1 << apart) for i in range(lax.axis_size(a...  118 us
    reduce_scatter x1, waiting for transfers between devices, local(): lax.psum_scatter(lax.dot_general(down_weight_codes, rotated, (((0,), (1,)...  82.7 us
    all_gather x1, waiting for transfers between devices, local(): lax.all_gather(adapter_input_factors, 'dp', axis=1, tiled=True)  38.9 us
    all_gather x1, waiting for transfers between devices, local(): piece = lax.all_gather(tokens, 'tensor', axis=1, tiled=True)  26.6 us
    all_gather x1, waiting for transfers between devices, local(): lax.all_gather(adapter_output_factors, 'dp', axis=1, tiled=True)  20.2 us
    convert_element_type x1, local copies, waits for them, and re-layouts, local(): local_table = (outer_table[:, None, :, None] * inner_table[None, :, None,...  13.6 us
    add x1, other arithmetic, local(): row_adapter_entry // slot_count * group_adapters  9.86 us
    ppermute x4, starting transfers between devices, from_partner(): lax.ppermute(x, axis, [(i, i ^ 1 << apart) for i in range(lax.axis_size(a...  9.71 us
  transfers between devices with their start and end apart: 8, of which 8 were waited for; matrix products, arithmetic and copies ran while one was open for 14% of the time, Pallas kernels for 0%

commit v1 on v0

v1 whole, which is shorter than its diff:
```python
import functools
import math

import jax
import jax.numpy as jnp
import numpy as np
from jax import lax
from jax.experimental import pallas as pl
from jax.experimental.pallas import tpu as pltpu
from jax.sharding import PartitionSpec as P

HIDDEN_UNITS = 14336
RANK = 16
SIDE = 4
TENSOR = SIDE * SIDE
GROUPS = 8
SLOTS = 2
QUARTERS = 4
MIB = 1024 * 1024


def steps(a):
    return min(a, SIDE - a)


def depth(o):
    return steps(o[0]) + steps(o[1])


OFFSETS = sorted(((a, b) for a in range(SIDE) for b in range(SIDE)), key=depth)
ORDER = {o: i for i, o in enumerate(OFFSETS)}


def parent(q, o):
    dz, dy = o
    via = 1 if q % 2 == 0 else SIDE - 1

    def back(a):
        return via if a == 2 else 0

    if q < 2:
        return (dz, back(dy)) if dy else (back(dz), 0)
    return (back(dz), dy) if dz else (0, back(dy))


CHILDREN = {
    (q, o): [c for c in OFFSETS if c != (0, 0) and parent(q, c) == o]
    for q in range(QUARTERS)
    for o in OFFSETS
}


def rotation_table(local_units):
    order = local_units // 28
    index = np.arange(order)
    walsh = np.ones((order, order), np.int64)
    for bit in range(max(order.bit_length() - 1, 0)):
        walsh *= 1 - 2 * ((index[:, None] & index[None, :]) >> bit & 1)
    conference = np.ones((14, 14), np.int64)
    residues = {j * j % 13 for j in range(1, 13)}
    conference[0, 0] = 0
    for i in range(13):
        for j in range(13):
            offset = (j - i) % 13
            conference[i + 1, j + 1] = 0 if offset == 0 else (1 if offset in residues else -1)
    paley = np.kron(conference, np.array([[1, 1], [1, -1]])) + np.kron(
        np.eye(14, dtype=np.int64), np.array([[1, -1], [-1, -1]])
    )
    return np.kron(walsh, paley).astype(np.float32)


def body(
    tokens, wg, wu, wd, gs, us, ds, fa, fb, lists, entry, table, out,
    xs, wv, wdv, tv, acc, hid, gst, ra, rb, rot, rotc, part, rss, rsr,
    fav, fbv, stage, fac, lrz, lry, low,
    own_sem, w_sem, misc_sem, ag_s, ag_r, dp_s, dp_r, lz_s, lz_r, ly_s, ly_r,
    a1_s, a1_r, a2_s, a2_r, rs_s, rs_r,
):
    rows, width = tokens.shape
    units = wg.shape[1]
    quarter = rows // QUARTERS
    panels = units // 128
    share = ra.shape[1]
    d = lax.axis_index("dp")
    t = lax.axis_index("tensor")
    z = lax.div(t, SIDE)
    y = lax.rem(t, SIDE)

    def at(o, sign=1):
        return (
            lax.rem(z + sign * o[0] + SIDE, SIDE) * SIDE + lax.rem(y + sign * o[1] + SIDE, SIDE)
        )

    def remote(src, dst, send, recv, to, axis="tensor"):
        return pltpu.make_async_remote_copy(
            src_ref=src, dst_ref=dst, send_sem=send, recv_sem=recv,
            device_id={axis: to}, device_id_type=pl.DeviceIdType.MESH,
        )

    sent = []

    def send(*args, **kw):
        copy = remote(*args, **kw)
        copy.start()
        sent.append(copy)

    barrier = pltpu.get_barrier_semaphore()
    for o in OFFSETS[1:]:
        pl.semaphore_signal(
            barrier, inc=1, device_id={"tensor": at(o)}, device_id_type=pl.DeviceIdType.MESH
        )
    for i in range(1, GROUPS):
        pl.semaphore_signal(
            barrier, inc=1, device_id={"dp": lax.rem(d + i, GROUPS)},
            device_id_type=pl.DeviceIdType.MESH,
        )

    own = pltpu.make_async_copy(tokens, xs.at[t], own_sem)
    own.start()
    fa_copy = pltpu.make_async_copy(
        fa.at[pl.ds(pl.multiple_of(t * width, width), width), :], fav, misc_sem.at[0]
    )
    fa_copy.start()
    fb_copy = pltpu.make_async_copy(fb, fbv, misc_sem.at[1])
    fb_copy.start()
    w_copies = []
    for i, o in enumerate(OFFSETS):
        block = pl.ds(pl.multiple_of(at(o, -1) * width, width), width)
        pair = (
            pltpu.make_async_copy(wg.at[block, :], wv.at[i, :, 0:units], w_sem.at[i, 0]),
            pltpu.make_async_copy(wu.at[block, :], wv.at[i, :, units : 2 * units], w_sem.at[i, 1]),
        )
        for copy in pair:
            copy.start()
        w_copies.append(pair)
    table_copy = pltpu.make_async_copy(table, tv, misc_sem.at[2])
    table_copy.start()
    wd_copy = pltpu.make_async_copy(wd, wdv, misc_sem.at[3])
    wd_copy.start()

    fa_copy.wait()
    fb_copy.wait()
    rank_row = lax.broadcasted_iota(jnp.int32, (RANK, GROUPS * RANK), 0)
    column = lax.broadcasted_iota(jnp.int32, (RANK, GROUPS * RANK), 1)
    picks = []
    for g in range(GROUPS):
        for s in range(SLOTS):
            picked = lists[g * GROUPS * SLOTS + d * SLOTS + s]
            picks.append((column == picked * RANK + rank_row).astype(jnp.float32))
    pick = jnp.concatenate(picks, axis=0).astype(jnp.bfloat16)
    nt = (((1,), (1,)), ((), ()))
    stage[:, 0:width] = lax.dot_general(
        pick, fav[...], nt, preferred_element_type=jnp.float32
    ).astype(jnp.bfloat16)
    stage[:, width:] = lax.dot_general(
        pick, fbv[...], nt, preferred_element_type=jnp.float32
    ).astype(jnp.bfloat16)
    block_rows = SLOTS * RANK
    mine = pl.ds(pl.multiple_of(d * block_rows, block_rows), block_rows)
    fac[mine, :] = stage[mine, :]

    pl.semaphore_wait(barrier, TENSOR - 1 + GROUPS - 1)

    def rows_of(q):
        return pl.ds(q * quarter, quarter)

    def forward(q, o):
        source = at(o, -1)
        for c in CHILDREN[q, o]:
            hop = (c[0] - o[0], c[1] - o[1])
            src = tokens.at[rows_of(q), :] if o == (0, 0) else xs.at[source, rows_of(q), :]
            send(
                src, xs.at[source, rows_of(q), :],
                ag_s.at[q, ORDER[c]], ag_r.at[q, ORDER[c]], at(hop),
            )

    def arrived(q, o):
        source = at(o, -1)
        slot = xs.at[source, rows_of(q), :]
        remote(slot, slot, ag_s.at[q, ORDER[o]], ag_r.at[q, ORDER[o]], source).wait_recv()

    def multiply(i, o):
        source = at(o, -1)
        for copy in w_copies[i]:
            copy.wait()

        @pl.loop(0, 2 * units // 256)
        def _(n):
            columns = pl.ds(pl.multiple_of(n * 256, 256), 256)
            product = jnp.dot(
                xs[source], wv[i, :, columns], preferred_element_type=jnp.float32
            )
            if i == 0:
                acc[:, columns] = product
            else:
                acc[:, columns] += product

    for q in range(QUARTERS):
        forward(q, (0, 0))
    for i in range(1, GROUPS):
        peer = lax.rem(d + i, GROUPS)
        theirs = pl.ds(pl.multiple_of(peer * block_rows, block_rows), block_rows)
        send(stage.at[theirs, :], fac.at[mine, :], dp_s.at[i], dp_r.at[i], peer, axis="dp")
    own.wait()
    multiply(0, (0, 0))

    slot_of = lax.broadcasted_iota(jnp.int32, (GROUPS * SLOTS * RANK, rows), 0) // RANK
    chosen = slot_of == entry[...]

    def low_partial():
        for i in range(1, GROUPS):
            peer = lax.rem(d - i + GROUPS, GROUPS)
            theirs = pl.ds(pl.multiple_of(peer * block_rows, block_rows), block_rows)
            slot = fac.at[theirs, :]
            remote(slot, slot, dp_s.at[i], dp_r.at[i], peer, axis="dp").wait_recv()
        everyone = lax.dot_general(
            fac[:, 0:width], xs[t], nt, preferred_element_type=jnp.float32
        )
        kept = jnp.where(chosen, everyone, 0.0)
        lrz[0] = jnp.sum(kept.reshape(GROUPS * SLOTS, RANK, rows), axis=0)
        for i in range(1, SIDE):
            send(lrz.at[0], lrz.at[i], lz_s.at[i], lz_r.at[i], at((i, 0)))

    def low_along_y():
        for i in range(1, SIDE):
            remote(lrz.at[i], lrz.at[i], lz_s.at[i], lz_r.at[i], at((i, 0), -1)).wait_recv()
        lry[0] = (lrz[0] + lrz[1]) + (lrz[2] + lrz[3])
        for i in range(1, SIDE):
            send(lry.at[0], lry.at[i], ly_s.at[i], ly_r.at[i], at((0, i)))

    def low_whole():
        for i in range(1, SIDE):
            remote(lry.at[i], lry.at[i], ly_s.at[i], ly_r.at[i], at((0, i), -1)).wait_recv()
        total = (lry[0] + lry[1]) + (lry[2] + lry[3])
        total = total.astype(jnp.bfloat16).astype(jnp.float32)
        spread = jnp.concatenate([total] * (GROUPS * SLOTS), axis=0)
        low[...] = jnp.transpose(jnp.where(chosen, spread, 0.0)).astype(jnp.bfloat16)

    after = {4: low_partial, 10: low_along_y, 14: low_whole}
    for i, o in enumerate(OFFSETS):
        if i == 0:
            continue
        for q in range(QUARTERS):
            arrived(q, o)
            forward(q, o)
        multiply(i, o)
        if i in after:
            after[i]()

    @pl.loop(0, panels)
    def _(j):
        columns = pl.ds(pl.multiple_of(j * 128, 128), 128)
        up_columns = pl.ds(pl.multiple_of(units + j * 128, 128), 128)
        factor_columns = pl.ds(pl.multiple_of(width + j * 128, 128), 128)
        gate = acc[:, columns] * gs[:, columns]
        extra = jnp.dot(low[...], fac[:, factor_columns], preferred_element_type=jnp.float32)
        up = acc[:, up_columns] * us[:, columns] + extra
        hid[:, columns] = (gate / (1.0 + jnp.exp(-gate)) * up).astype(jnp.bfloat16)

    table_copy.wait()
    for j in range(0, panels, 2):
        wide = min(2, panels - j)
        turned = jnp.dot(
            hid[...], tv[:, j * 128 : (j + wide) * 128], preferred_element_type=jnp.float32
        ).astype(jnp.bfloat16)
        for k in range(wide):
            gst[(j + k) * rows : (j + k + 1) * rows, :] = turned[:, k * 128 : (k + 1) * 128]
    gst[panels * rows :, :] = jnp.zeros((gst.shape[0] - panels * rows, 128), jnp.bfloat16)

    def share_of(index):
        return pl.ds(pl.multiple_of(index * share, 16), share)

    far_first = OFFSETS[:0:-1]
    for o in far_first:
        i = ORDER[o]
        peer = at(o)
        send(gst.at[share_of(peer), :], ra.at[t], a1_s.at[i], a1_r.at[i], peer)
    ra[t] = gst[share_of(t), :]
    for o in far_first[::-1]:
        i = ORDER[o]
        peer = at(o, -1)
        remote(ra.at[peer], ra.at[peer], a1_s.at[i], a1_r.at[i], peer).wait_recv()
    norm = 1.0 / math.sqrt(HIDDEN_UNITS)

    @pl.loop(0, share // 16)
    def _(k):
        tile = pl.ds(pl.multiple_of(k * 16, 16), 16)
        terms = [ra[i, tile, :].astype(jnp.float32) for i in range(TENSOR)]
        for bit in range(4):
            mixed = list(terms)
            for i in range(TENSOR):
                j = i ^ (1 << bit)
                if i < j:
                    mixed[i] = terms[i] + terms[j]
                    mixed[j] = terms[i] - terms[j]
            terms = mixed
        for i in range(TENSOR):
            rb[i, tile, :] = (terms[i] * norm).astype(jnp.bfloat16)

    for o in far_first:
        i = ORDER[o]
        peer = at(o)
        send(rb.at[peer], rot.at[share_of(t), :], a2_s.at[i], a2_r.at[i], peer)
    rot[share_of(t), :] = rb[t]
    for o in far_first[::-1]:
        i = ORDER[o]
        peer = at(o, -1)
        slot = rot.at[share_of(peer), :]
        remote(slot, slot, a2_s.at[i], a2_r.at[i], peer).wait_recv()
    for j in range(panels):
        rotc[:, j * 128 : (j + 1) * 128] = rot[j * rows : (j + 1) * rows, :]

    wd_copy.wait()

    def project(o):
        target = at(o, -1)
        columns = pl.ds(pl.multiple_of(target * width, width), width)
        part[ORDER[o]] = jnp.dot(
            rotc[...], wdv[:, columns], preferred_element_type=jnp.float32
        )

    def collected(q, o):
        total = part[ORDER[o], rows_of(q), :]
        for c in CHILDREN[q, o]:
            slot = rsr.at[ORDER[c], rows_of(q), :]
            remote(slot, slot, rs_s.at[q, ORDER[c]], rs_r.at[q, ORDER[c]], t).wait_recv()
            total = total + rsr[ORDER[c], rows_of(q), :].astype(jnp.float32)
        return total

    def pass_up(q, o):
        rss[ORDER[o], rows_of(q), :] = collected(q, o).astype(jnp.bfloat16)
        above = parent(q, o)
        hop = (above[0] - o[0], above[1] - o[1])
        send(
            rss.at[ORDER[o], rows_of(q), :], rsr.at[ORDER[o], rows_of(q), :],
            rs_s.at[q, ORDER[o]], rs_r.at[q, ORDER[o]], at(hop),
        )

    for level in (4, 3, 2, 1):
        here = [o for o in OFFSETS if depth(o) == level]
        for o in here:
            project(o)
            for q in range(QUARTERS):
                if not CHILDREN[q, o]:
                    pass_up(q, o)
        if level == 1:
            project((0, 0))
        for o in here:
            for q in range(QUARTERS):
                if CHILDREN[q, o]:
                    pass_up(q, o)
    for q in range(QUARTERS):
        out[rows_of(q), :] = (collected(q, (0, 0)) * ds[...]).astype(jnp.bfloat16)
    for copy in sent:
        copy.wait_send()


def local(
    tokens,
    gate_weight_codes,
    up_weight_codes,
    down_weight_codes,
    gate_channel_scale,
    up_channel_scale,
    down_channel_scale,
    adapter_input_factors,
    adapter_output_factors,
    group_adapter_lists,
    row_adapter_entry,
):
    rows, width = tokens.shape
    units = gate_weight_codes.shape[1]
    factors = adapter_input_factors.shape[1]
    picked = GROUPS * SLOTS * RANK
    panels = units // 128
    share = -(-panels * rows // (16 * TENSOR)) * 16
    bf16, f32 = jnp.bfloat16, jnp.float32
    table = jnp.asarray(rotation_table(units), bf16)
    hbm = pl.BlockSpec(memory_space=pl.ANY)
    vmem = pl.BlockSpec(memory_space=pltpu.VMEM)
    smem = pl.BlockSpec(memory_space=pltpu.SMEM)
    dma = pltpu.SemaphoreType.DMA
    return pl.pallas_call(
        body,
        out_shape=jax.ShapeDtypeStruct((rows, width), bf16),
        in_specs=[hbm, hbm, hbm, hbm, vmem, vmem, vmem, hbm, hbm, smem, vmem, hbm],
        out_specs=vmem,
        scratch_shapes=[
            pltpu.VMEM((TENSOR, rows, width), bf16),
            pltpu.VMEM((TENSOR, width, 2 * units), bf16),
            pltpu.VMEM(down_weight_codes.shape, bf16),
            pltpu.VMEM((units, units), bf16),
            pltpu.VMEM((rows, 2 * units), f32),
            pltpu.VMEM((rows, units), bf16),
            pltpu.VMEM((TENSOR * share, 128), bf16),
            pltpu.VMEM((TENSOR, share, 128), bf16),
            pltpu.VMEM((TENSOR, share, 128), bf16),
            pltpu.VMEM((TENSOR * share, 128), bf16),
            pltpu.VMEM((rows, units), bf16),
            pltpu.VMEM((TENSOR, rows, width), f32),
            pltpu.VMEM((TENSOR, rows, width), bf16),
            pltpu.VMEM((TENSOR, rows, width), bf16),
            pltpu.VMEM((width, factors), bf16),
            pltpu.VMEM((units, factors), bf16),
            pltpu.VMEM((picked, width + units), bf16),
            pltpu.VMEM((picked, width + units), bf16),
            pltpu.VMEM((SIDE, RANK, rows), f32),
            pltpu.VMEM((SIDE, RANK, rows), f32),
            pltpu.VMEM((rows, picked), bf16),
            dma,
            dma((TENSOR, 2)),
            dma((4,)),
            dma((QUARTERS, TENSOR)),
            dma((QUARTERS, TENSOR)),
            dma((GROUPS,)),
            dma((GROUPS,)),
            dma((SIDE,)),
            dma((SIDE,)),
            dma((SIDE,)),
            dma((SIDE,)),
            dma((TENSOR,)),
            dma((TENSOR,)),
            dma((TENSOR,)),
            dma((TENSOR,)),
            dma((QUARTERS, TENSOR)),
            dma((QUARTERS, TENSOR)),
        ],
        compiler_params=pltpu.CompilerParams(
            collective_id=0, has_side_effects=True, vmem_limit_bytes=60 * MIB
        ),
    )(
        tokens,
        gate_weight_codes,
        up_weight_codes,
        down_weight_codes,
        gate_channel_scale.reshape(1, -1),
        up_channel_scale.reshape(1, -1),
        down_channel_scale.reshape(1, -1),
        adapter_input_factors,
        adapter_output_factors,
        group_adapter_lists.reshape(-1),
        row_adapter_entry.reshape(1, -1),
        table,
    )


def solution(mesh):
    return jax.shard_map(
        local,
        mesh=mesh,
        in_specs=(
            P("dp", "tensor"),
            P(None, "tensor"),
            P(None, "tensor"),
            P("tensor", None),
            P("tensor"),
            P("tensor"),
            P("tensor"),
            P(None, "dp"),
            P("tensor", "dp"),
            P(),
            P("dp"),
        ),
        out_specs=P("dp", "tensor"),
        check_vma=False,
    )
```

time: 385 us -> 92.8 us (0.24)
  waiting for transfers between devices: 289 us -> 0 us
  Pallas kernels: 0 us -> 85.7 us
  matrix products: 37.5 us -> 0 us
  other arithmetic: 21.3 us -> 0 us
  between operations: 13.3 us -> 0.01 us
  starting transfers between devices: 9.83 us -> 0 us
  local copies, waits for them, and re-layouts: 14.5 us -> 6.87 us
    ppermute x4 -> x0, waiting for transfers between devices: 118 us -> none  [from_partner(): lax.ppermute(x, axis, [(i, i ^ 1 << apart) for i in range(lax.axis_size(a...]
    pallas_call x0 -> x1, Pallas kernels: none -> 85.7 us  [local(): pl.pallas_call(body, out_shape=jax.ShapeDtypeStruct((rows, width), bf16),...]
    all_gather x3 -> x0, waiting for transfers between devices: 85.6 us -> none  [the longest x1 38.9 us: local(): lax.all_gather(adapter_input_factors, 'dp', axis=1, tiled=True)]
    reduce_scatter x1 -> x0, waiting for transfers between devices: 82.7 us -> none  [local(): lax.psum_scatter(lax.dot_general(down_weight_codes, rotated, (((0,), (1,)...]
    dot_general x5 -> x0, matrix products: 37.5 us -> none  [the longest x1 8.71 us: local(): up_raw = jnp.dot(piece, up_weight_codes, preferred_element_type=jnp.float32)]
    convert_element_type x1 -> x0, local copies, waits for them, and re-layouts: 13.6 us -> none  [local(): local_table = (outer_table[:, None, :, None] * inner_table[None, :, None,...]
    add x2 -> x0, other arithmetic: 9.96 us -> none  [the longest x1 9.86 us: local(): row_adapter_entry // slot_count * group_adapters]
    ppermute x4 -> x0, starting transfers between devices: 9.71 us -> none  [from_partner(): lax.ppermute(x, axis, [(i, i ^ 1 << apart) for i in range(lax.axis_size(a...]
  transfers between devices with their start and end apart: 8 -> 0, of which waited for: 8 -> 0; matrix products, arithmetic and copies ran while one was open for 14% -> 0% of each run, Pallas kernels for 0% -> 0%
where the time goes in v1:
time: 92.8 us; the launch traced here: 92.5 us
  Pallas kernels  85.7 us (92%)
  local copies, waits for them, and re-layouts  6.87 us (7%)
    pallas_call x1, Pallas kernels, local(): pl.pallas_call(body, out_shape=jax.ShapeDtypeStruct((rows, width), bf16),...  85.7 us
    unnamed x2, local copies, waits for them, and re-layouts  2.43 us

profile of v1, /device:TPU:0, one launch (start us, length us, event | category | flops | bytes accessed | tf_op | source)
XLA Modules:
  0.0 92.5 jit_solution(12881318463880595637)
XLA Ops:
  0.0 1.2 %reshape.19.entry = s32[1,384]{1,0:T(1,128)} reshape(s32[384]{0:T(512)} %param.22) | data formatting | bytes 3072 | tf_op jit(solution)/shard_map/reshape | solution.py:442
  1.2 1.3 %reshape.15.gs = f32[1,896]{1,0:T(1,128)} reshape(f32[896]{0:T(1024)} %param.16) | data formatting | bytes 7168 | tf_op jit(solution)/shard_map/reshape | solution.py:436
  2.5 1.3 %reshape.16.us = f32[1,896]{1,0:T(1,128)} reshape(f32[896]{0:T(1024)} %param.17) | data formatting | bytes 7168 | tf_op jit(solution)/shard_map/reshape | solution.py:437
  3.8 0.8 copy.14
  4.6 0.7 reshape.18.lists
  5.3 85.7 %shard_map.118 = bf16[384,256]{1,0:T(8,128)(2,1)} custom-call(bf16[384,256]{1,0:T(8,128)(2,1)} %tokens.1, bf16[4096,896]{1,0:T(8,128)(2,1)} %wg.1, bf16[4096,896]{1,0:T(8,128)(2,1)} %wu.1, bf16[896,4096]{1,0:T(8,128)(2,1)} %wd.1, f32[1,896]{1,0:T(1,128)} %reshape.15.gs, f32[1,896]{1,0:T(1,128)} %reshape.16.us, f32[1,256]{1,0:T(1,128)} %bitcast.1, ...), custom_call_target="tpu_custom_call" | custom-call | tf_op jit(solution)/shard_map/pallas_call | solution.py:383
  90.9 1.6 %copy.16 = bf16[384,256]{1,0:T(8,128)(2,1)} copy(bf16[384,256]{1,0:T(8,128)(2,1)} %shard_map.118) | data formatting | bytes 393216

commit v2 on v1

--- a/solution.py
+++ b/solution.py
@@ -28,6 +28,7 @@
 
 
 OFFSETS = sorted(((a, b) for a in range(SIDE) for b in range(SIDE)), key=depth)
+LEVELS = [[o for o in OFFSETS if depth(o) == level] for level in range(5)]
 ORDER = {o: i for i, o in enumerate(OFFSETS)}
 
 
@@ -97,15 +98,14 @@
             device_id={axis: to}, device_id_type=pl.DeviceIdType.MESH,
         )
 
-    sent = []
-
     def send(*args, **kw):
-        copy = remote(*args, **kw)
-        copy.start()
-        sent.append(copy)
+        remote(*args, **kw).start()
+
+    def received(like, semaphore):
+        pltpu.make_async_copy(like, like, semaphore).wait()
 
     barrier = pltpu.get_barrier_semaphore()
-    for o in OFFSETS[1:]:
+    for o in LEVELS[1]:
         pl.semaphore_signal(
             barrier, inc=1, device_id={"tensor": at(o)}, device_id_type=pl.DeviceIdType.MESH
         )
@@ -123,16 +123,10 @@
     fa_copy.start()
     fb_copy = pltpu.make_async_copy(fb, fbv, misc_sem.at[1])
     fb_copy.start()
-    w_copies = []
     for i, o in enumerate(OFFSETS):
         block = pl.ds(pl.multiple_of(at(o, -1) * width, width), width)
-        pair = (
-            pltpu.make_async_copy(wg.at[block, :], wv.at[i, :, 0:units], w_sem.at[i, 0]),
-            pltpu.make_async_copy(wu.at[block, :], wv.at[i, :, units : 2 * units], w_sem.at[i, 1]),
-        )
-        for copy in pair:
-            copy.start()
-        w_copies.append(pair)
+        pltpu.make_async_copy(wg.at[block, :], wv.at[i, :, 0:units], w_sem.at[i]).start()
+        pltpu.make_async_copy(wu.at[block, :], wv.at[i, :, units : 2 * units], w_sem.at[i]).start()
     table_copy = pltpu.make_async_copy(table, tv, misc_sem.at[2])
     table_copy.start()
     wd_copy = pltpu.make_async_copy(wd, wdv, misc_sem.at[3])
@@ -145,7 +139,7 @@
     picks = []
     for g in range(GROUPS):
         for s in range(SLOTS):
-            picked = lists[g * GROUPS * SLOTS + d * SLOTS + s]
+            picked = lists[g, s, d]
             picks.append((column == picked * RANK + rank_row).astype(jnp.float32))
     pick = jnp.concatenate(picks, axis=0).astype(jnp.bfloat16)
     nt = (((1,), (1,)), ((), ()))
@@ -159,7 +153,7 @@
     mine = pl.ds(pl.multiple_of(d * block_rows, block_rows), block_rows)
     fac[mine, :] = stage[mine, :]
 
-    pl.semaphore_wait(barrier, TENSOR - 1 + GROUPS - 1)
+    pl.semaphore_wait(barrier, len(LEVELS[1]) + GROUPS - 1)
 
     def rows_of(q):
         return pl.ds(q * quarter, quarter)
@@ -171,18 +165,15 @@
             src = tokens.at[rows_of(q), :] if o == (0, 0) else xs.at[source, rows_of(q), :]
             send(
                 src, xs.at[source, rows_of(q), :],
-                ag_s.at[q, ORDER[c]], ag_r.at[q, ORDER[c]], at(hop),
+                ag_s, ag_r.at[q, depth(c)], at(hop),
             )
 
-    def arrived(q, o):
-        source = at(o, -1)
-        slot = xs.at[source, rows_of(q), :]
-        remote(slot, slot, ag_s.at[q, ORDER[o]], ag_r.at[q, ORDER[o]], source).wait_recv()
+    def arrived(q, level):
+        received(xs.at[0 : len(LEVELS[level]), rows_of(q), :], ag_r.at[q, level])
 
     def multiply(i, o):
         source = at(o, -1)
-        for copy in w_copies[i]:
-            copy.wait()
+        received(wv.at[i], w_sem.at[i])
 
         @pl.loop(0, 2 * units // 256)
         def _(n):
@@ -200,61 +191,61 @@
     for i in range(1, GROUPS):
         peer = lax.rem(d + i, GROUPS)
         theirs = pl.ds(pl.multiple_of(peer * block_rows, block_rows), block_rows)
-        send(stage.at[theirs, :], fac.at[mine, :], dp_s.at[i], dp_r.at[i], peer, axis="dp")
+        send(stage.at[theirs, :], fac.at[mine, :], dp_s, dp_r, peer, axis="dp")
     own.wait()
-    multiply(0, (0, 0))
 
     slot_of = lax.broadcasted_iota(jnp.int32, (GROUPS * SLOTS * RANK, rows), 0) // RANK
-    chosen = slot_of == entry[...]
+    chosen = slot_of == entry[...].reshape(1, rows)
 
     def low_partial():
-        for i in range(1, GROUPS):
-            peer = lax.rem(d - i + GROUPS, GROUPS)
-            theirs = pl.ds(pl.multiple_of(peer * block_rows, block_rows), block_rows)
-            slot = fac.at[theirs, :]
-            remote(slot, slot, dp_s.at[i], dp_r.at[i], peer, axis="dp").wait_recv()
+        received(fac.at[0 : (GROUPS - 1) * block_rows], dp_r)
         everyone = lax.dot_general(
             fac[:, 0:width], xs[t], nt, preferred_element_type=jnp.float32
         )
         kept = jnp.where(chosen, everyone, 0.0)
         lrz[0] = jnp.sum(kept.reshape(GROUPS * SLOTS, RANK, rows), axis=0)
         for i in range(1, SIDE):
-            send(lrz.at[0], lrz.at[i], lz_s.at[i], lz_r.at[i], at((i, 0)))
+            send(lrz.at[0], lrz.at[i], lz_s, lz_r, at((i, 0)))
 
     def low_along_y():
-        for i in range(1, SIDE):
-            remote(lrz.at[i], lrz.at[i], lz_s.at[i], lz_r.at[i], at((i, 0), -1)).wait_recv()
+        received(lrz.at[1:], lz_r)
         lry[0] = (lrz[0] + lrz[1]) + (lrz[2] + lrz[3])
         for i in range(1, SIDE):
-            send(lry.at[0], lry.at[i], ly_s.at[i], ly_r.at[i], at((0, i)))
+            send(lry.at[0], lry.at[i], ly_s, ly_r, at((0, i)))
 
     def low_whole():
-        for i in range(1, SIDE):
-            remote(lry.at[i], lry.at[i], ly_s.at[i], ly_r.at[i], at((0, i), -1)).wait_recv()
+        received(lry.at[1:], ly_r)
         total = (lry[0] + lry[1]) + (lry[2] + lry[3])
         total = total.astype(jnp.bfloat16).astype(jnp.float32)
         spread = jnp.concatenate([total] * (GROUPS * SLOTS), axis=0)
         low[...] = jnp.transpose(jnp.where(chosen, spread, 0.0)).astype(jnp.bfloat16)
 
-    after = {4: low_partial, 10: low_along_y, 14: low_whole}
-    for i, o in enumerate(OFFSETS):
-        if i == 0:
-            continue
+    work = [lambda: multiply(0, (0, 0))]
+    for level in range(1, 5):
+        ready = len(work)
         for q in range(QUARTERS):
-            arrived(q, o)
-            forward(q, o)
-        multiply(i, o)
-        if i in after:
-            after[i]()
+            arrived(q, level)
+            for o in LEVELS[level]:
+                forward(q, o)
+            for _ in range(-(-ready // QUARTERS)):
+                if ready:
+                    work.pop(0)()
+                    ready -= 1
+        for o in LEVELS[level]:
+            work.append(functools.partial(multiply, ORDER[o], o))
+        if level < 4:
+            work.insert(2, (low_partial, low_along_y, low_whole)[level - 1])
+    for item in work:
+        item()
 
     @pl.loop(0, panels)
     def _(j):
         columns = pl.ds(pl.multiple_of(j * 128, 128), 128)
         up_columns = pl.ds(pl.multiple_of(units + j * 128, 128), 128)
         factor_columns = pl.ds(pl.multiple_of(width + j * 128, 128), 128)
-        gate = acc[:, columns] * gs[:, columns]
+        gate = acc[:, columns] * gs[columns].reshape(1, 128)
         extra = jnp.dot(low[...], fac[:, factor_columns], preferred_element_type=jnp.float32)
-        up = acc[:, up_columns] * us[:, columns] + extra
+        up = acc[:, up_columns] * us[columns].reshape(1, 128) + extra
         hid[:, columns] = (gate / (1.0 + jnp.exp(-gate)) * up).astype(jnp.bfloat16)
 
     table_copy.wait()
@@ -272,14 +263,10 @@
 
     far_first = OFFSETS[:0:-1]
     for o in far_first:
-        i = ORDER[o]
         peer = at(o)
-        send(gst.at[share_of(peer), :], ra.at[t], a1_s.at[i], a1_r.at[i], peer)
+        send(gst.at[share_of(peer), :], ra.at[t], a1_s, a1_r, peer)
     ra[t] = gst[share_of(t), :]
-    for o in far_first[::-1]:
-        i = ORDER[o]
-        peer = at(o, -1)
-        remote(ra.at[peer], ra.at[peer], a1_s.at[i], a1_r.at[i], peer).wait_recv()
+    received(ra.at[1:], a1_r)
     norm = 1.0 / math.sqrt(HIDDEN_UNITS)
 
     @pl.loop(0, share // 16)
@@ -298,15 +285,10 @@
             rb[i, tile, :] = (terms[i] * norm).astype(jnp.bfloat16)
 
     for o in far_first:
-        i = ORDER[o]
         peer = at(o)
-        send(rb.at[peer], rot.at[share_of(t), :], a2_s.at[i], a2_r.at[i], peer)
+        send(rb.at[peer], rot.at[share_of(t), :], a2_s, a2_r, peer)
     rot[share_of(t), :] = rb[t]
-    for o in far_first[::-1]:
-        i = ORDER[o]
-        peer = at(o, -1)
-        slot = rot.at[share_of(peer), :]
-        remote(slot, slot, a2_s.at[i], a2_r.at[i], peer).wait_recv()
+    received(rot.at[share:, :], a2_r)
     for j in range(panels):
         rotc[:, j * 128 : (j + 1) * 128] = rot[j * rows : (j + 1) * rows, :]
 
@@ -322,8 +304,6 @@
     def collected(q, o):
         total = part[ORDER[o], rows_of(q), :]
         for c in CHILDREN[q, o]:
-            slot = rsr.at[ORDER[c], rows_of(q), :]
-            remote(slot, slot, rs_s.at[q, ORDER[c]], rs_r.at[q, ORDER[c]], t).wait_recv()
             total = total + rsr[ORDER[c], rows_of(q), :].astype(jnp.float32)
         return total
 
@@ -333,26 +313,33 @@
         hop = (above[0] - o[0], above[1] - o[1])
         send(
             rss.at[ORDER[o], rows_of(q), :], rsr.at[ORDER[o], rows_of(q), :],
-            rs_s.at[q, ORDER[o]], rs_r.at[q, ORDER[o]], at(hop),
+            rs_s, rs_r.at[q, depth(o)], at(hop),
         )
 
     for level in (4, 3, 2, 1):
-        here = [o for o in OFFSETS if depth(o) == level]
-        for o in here:
+        for o in LEVELS[level]:
             project(o)
             for q in range(QUARTERS):
                 if not CHILDREN[q, o]:
                     pass_up(q, o)
         if level == 1:
             project((0, 0))
-        for o in here:
+        if level < 4:
             for q in range(QUARTERS):
-                if CHILDREN[q, o]:
-                    pass_up(q, o)
+                received(rsr.at[0 : len(LEVELS[level + 1]), rows_of(q), :], rs_r.at[q, level + 1])
+                for o in LEVELS[level]:
+                    if CHILDREN[q, o]:
+                        pass_up(q, o)
     for q in range(QUARTERS):
-        out[rows_of(q), :] = (collected(q, (0, 0)) * ds[...]).astype(jnp.bfloat16)
-    for copy in sent:
-        copy.wait_send()
+        received(rsr.at[0 : len(LEVELS[1]), rows_of(q), :], rs_r.at[q, 1])
+        out[rows_of(q), :] = (collected(q, (0, 0)) * ds[...].reshape(1, width)).astype(jnp.bfloat16)
+    received(xs.at[0 : TENSOR - 1], ag_s)
+    received(fac.at[0 : (GROUPS - 1) * block_rows], dp_s)
+    received(lrz.at[1:], lz_s)
+    received(lry.at[1:], ly_s)
+    received(ra.at[1:], a1_s)
+    received(ra.at[1:], a2_s)
+    received(rss.at[1:], rs_s)
 
 
 def local(
@@ -408,22 +395,22 @@
             pltpu.VMEM((SIDE, RANK, rows), f32),
             pltpu.VMEM((rows, picked), bf16),
             dma,
-            dma((TENSOR, 2)),
+            dma((TENSOR,)),
             dma((4,)),
-            dma((QUARTERS, TENSOR)),
-            dma((QUARTERS, TENSOR)),
-            dma((GROUPS,)),
-            dma((GROUPS,)),
-            dma((SIDE,)),
-            dma((SIDE,)),
-            dma((SIDE,)),
-            dma((SIDE,)),
-            dma((TENSOR,)),
-            dma((TENSOR,)),
-            dma((TENSOR,)),
-            dma((TENSOR,)),
-            dma((QUARTERS, TENSOR)),
-            dma((QUARTERS, TENSOR)),
+            dma,
+            dma((QUARTERS, 5)),
+            dma,
+            dma,
+            dma,
+            dma,
+            dma,
+            dma,
+            dma,
+            dma,
+            dma,
+            dma,
+            dma,
+            dma((QUARTERS, 5)),
         ],
         compiler_params=pltpu.CompilerParams(
             collective_id=0, has_side_effects=True, vmem_limit_bytes=60 * MIB
@@ -433,13 +420,13 @@
         gate_weight_codes,
         up_weight_codes,
         down_weight_codes,
-        gate_channel_scale.reshape(1, -1),
-        up_channel_scale.reshape(1, -1),
-        down_channel_scale.reshape(1, -1),
+        gate_channel_scale,
+        up_channel_scale,
+        down_channel_scale,
         adapter_input_factors,
         adapter_output_factors,
-        group_adapter_lists.reshape(-1),
-        row_adapter_entry.reshape(1, -1),
+        jnp.transpose(group_adapter_lists, (0, 2, 1)),
+        row_adapter_entry,
         table,
     )
 

time: 92.8 us -> 86.7 us (0.934)
  local copies, waits for them, and re-layouts: 6.87 us -> 1.62 us
    reshape x4 -> x0, local copies, waits for them, and re-layouts: 4.44 us -> none  [the longest x1 1.27 us: local(): up_channel_scale.reshape(1, -1)]
    unnamed x2 -> x1, local copies, waits for them, and re-layouts: 2.43 us -> 1.62 us
where the time goes in v2:
time: 86.7 us; the launch traced here: 86.5 us
  Pallas kernels  84.9 us (98%)
  local copies, waits for them, and re-layouts  1.62 us (2%)
    pallas_call x1, Pallas kernels, local(): pl.pallas_call(body, out_shape=jax.ShapeDtypeStruct((rows, width), bf16),...  84.9 us

profile of v2, /device:TPU:0, one launch (start us, length us, event | category | flops | bytes accessed | tf_op | source)
XLA Modules:
  0.0 86.5 jit_solution(8216972955466978449)
XLA Ops:
  0.0 84.9 %shard_map.118 = bf16[384,256]{1,0:T(8,128)(2,1)} custom-call(bf16[384,256]{1,0:T(8,128)(2,1)} %tokens.1, bf16[4096,896]{1,0:T(8,128)(2,1)} %wg.1, bf16[4096,896]{1,0:T(8,128)(2,1)} %wu.1, bf16[896,4096]{1,0:T(8,128)(2,1)} %wd.1, f32[896]{0:T(1024)} %gs.1, f32[896]{0:T(1024)} %us.1, f32[256]{0:T(256)} %ds.1, bf16[4096,128]{1,0:T(8,128)(2,1)} %fa.1, ...), custom_call_target="tpu_custom_call" | custom-call | tf_op jit(solution)/shard_map/pallas_call | solution.py:370
  84.9 1.6 %copy.14 = bf16[384,256]{1,0:T(8,128)(2,1)} copy(bf16[384,256]{1,0:T(8,128)(2,1)} %shard_map.118) | data formatting | bytes 393216

commit v3 on v2

v3 whole, which is shorter than its diff:
```python
import functools
import math

import jax
import jax.numpy as jnp
import numpy as np
from jax import lax
from jax.experimental import pallas as pl
from jax.experimental.pallas import tpu as pltpu
from jax.sharding import PartitionSpec as P

HIDDEN_UNITS = 14336
RANK = 16
SIDE = 4
TENSOR = SIDE * SIDE
GROUPS = 8
SLOTS = 2
QUARTERS = 4
PARTS = ((0, 208), (208, 176))
TREES = ((0, 2), (1, 3))
TREE_ROWS = {0: (0, 96), 2: (96, 112), 1: (208, 96), 3: (304, 80)}
MIB = 1024 * 1024


def steps(a):
    return min(a, SIDE - a)


def depth(o):
    return steps(o[0]) + steps(o[1])


OFFSETS = sorted(((a, b) for a in range(SIDE) for b in range(SIDE)), key=depth)
ORDER = {o: i for i, o in enumerate(OFFSETS)}
NEAR = [o for o in OFFSETS if depth(o) == 1]
OPPOSITE = [(2, 0), (0, 2)]


def parent(q, o):
    dz, dy = o
    via = 1 if q % 2 == 0 else SIDE - 1
    if q < 2:
        return (dz, via if dy == 2 else 0) if dy else (0, 0)
    return (via if dz == 2 else 0, dy) if dz else (0, 0)


def level_of(q, o):
    return 0 if o == (0, 0) else 1 + level_of(q, parent(q, o))


LEVELS = {
    (q, level): [o for o in OFFSETS if level_of(q, o) == level]
    for q in range(QUARTERS)
    for level in range(5)
}
CHILDREN = {
    (q, o): [c for c in OFFSETS if c != (0, 0) and parent(q, c) == o]
    for q in range(QUARTERS)
    for o in OFFSETS
}
for children in CHILDREN.values():
    children.sort(key=depth, reverse=True)


def share_rows(rows, panels):
    return -(-panels * rows // (16 * TENSOR)) * 16


def rotation_table(local_units):
    order = local_units // 28
    index = np.arange(order)
    walsh = np.ones((order, order), np.int64)
    for bit in range(max(order.bit_length() - 1, 0)):
        walsh *= 1 - 2 * ((index[:, None] & index[None, :]) >> bit & 1)
    conference = np.ones((14, 14), np.int64)
    residues = {j * j % 13 for j in range(1, 13)}
    conference[0, 0] = 0
    for i in range(13):
        for j in range(13):
            offset = (j - i) % 13
            conference[i + 1, j + 1] = 0 if offset == 0 else (1 if offset in residues else -1)
    paley = np.kron(conference, np.array([[1, 1], [1, -1]])) + np.kron(
        np.eye(14, dtype=np.int64), np.array([[1, -1], [-1, -1]])
    )
    return np.kron(walsh, paley).astype(np.float32)


def body(
    tokens, wg, wu, wd, gs, us, ds, fa, fb, lists, entry, table, out,
    xs, wv, wdv, tv, acc, hid, gst, ra, rb, rot, rotc, part, rss, rsr,
    fav, fbv, stage, fac, relay, lrz, lry, low, extra,
    own_sem, w_sem, misc_sem, ag_s, ag_r, dp_s, dp_r, lz_s, lz_r, ly_s, ly_r,
    a1_s, a1_r, a2_s, a2_r, rs_s, rs_r,
):
    rows, width = tokens.shape
    units = wg.shape[1]
    panels = units // 128
    shares = [share_rows(count, panels) for _, count in PARTS]
    bases = [sum(shares[:p]) for p in range(len(PARTS))]
    d = lax.axis_index("dp")
    t = lax.axis_index("tensor")
    z = lax.div(t, SIDE)
    y = lax.rem(t, SIDE)

    def at(o, sign=1):
        return (
            lax.rem(z + sign * o[0] + SIDE, SIDE) * SIDE + lax.rem(y + sign * o[1] + SIDE, SIDE)
        )

    def remote(src, dst, send, recv, to, axis="tensor"):
        return pltpu.make_async_remote_copy(
            src_ref=src, dst_ref=dst, send_sem=send, recv_sem=recv,
            device_id={axis: to}, device_id_type=pl.DeviceIdType.MESH,
        )

    def send(*args, **kw):
        remote(*args, **kw).start()

    def received(like, semaphore):
        pltpu.make_async_copy(like, like, semaphore).wait()

    barrier = pltpu.get_barrier_semaphore()
    for o in NEAR + OPPOSITE:
        pl.semaphore_signal(
            barrier, inc=1, device_id={"tensor": at(o)}, device_id_type=pl.DeviceIdType.MESH
        )
    core = lax.rem(d, 2)
    partner = d + 1 - 2 * core
    along_x = [lax.rem(d + 2 * i, GROUPS) for i in range(1, SIDE)]
    for peer in [partner] + along_x:
        pl.semaphore_signal(
            barrier, inc=1, device_id={"dp": peer}, device_id_type=pl.DeviceIdType.MESH
        )

    own = pltpu.make_async_copy(tokens, xs.at[t], own_sem)
    own.start()
    fa_copy = pltpu.make_async_copy(
        fa.at[pl.ds(pl.multiple_of(t * width, width), width), :], fav, misc_sem.at[0]
    )
    fa_copy.start()
    fb_copy = pltpu.make_async_copy(fb, fbv, misc_sem.at[1])
    fb_copy.start()
    def fetch(first, count):
        for i in range(first, first + count):
            block = pl.ds(pl.multiple_of(at(OFFSETS[i], -1) * width, width), width)
            pltpu.make_async_copy(wg.at[block, :], wv.at[i, :, 0:units], w_sem.at[i]).start()
            pltpu.make_async_copy(
                wu.at[block, :], wv.at[i, :, units : 2 * units], w_sem.at[i]
            ).start()

    fetch(0, 5)
    table_copy = pltpu.make_async_copy(table, tv, misc_sem.at[2])
    wd_copy = pltpu.make_async_copy(wd, wdv, misc_sem.at[3])

    pl.semaphore_wait(barrier, len(NEAR) + len(OPPOSITE) + SIDE)

    def rows_of(q):
        return pl.ds(*TREE_ROWS[q])

    def part_rows(p):
        return pl.ds(*PARTS[p])

    def forward(q, o):
        source = at(o, -1)
        for c in CHILDREN[q, o]:
            hop = (c[0] - o[0], c[1] - o[1])
            src = tokens.at[rows_of(q), :] if o == (0, 0) else xs.at[source, rows_of(q), :]
            send(
                src, xs.at[source, rows_of(q), :],
                ag_s, ag_r.at[q, level_of(q, c)], at(hop),
            )

    def arrived(q, level):
        received(xs.at[0 : len(LEVELS[q, level]), rows_of(q), :], ag_r.at[q, level])

    def load(first, count):
        for i in range(first, first + count):
            received(wv.at[i], w_sem.at[i])

    def multiply(some, first, count):
        sources = [at(OFFSETS[i], -1) for i in range(first, first + count)]
        for n in range(2 * units // 256):
            columns = slice(n * 256, (n + 1) * 256)
            x = jnp.concatenate([xs[source, some, :] for source in sources], axis=1)
            w = wv[first : first + count, :, columns].reshape(count * width, 256)
            product = jnp.dot(x, w, preferred_element_type=jnp.float32)
            if first == 0:
                acc[some, columns] = product
            else:
                acc[some, columns] += product

    for q in TREE_ROWS:
        forward(q, (0, 0))
    fetch(5, 11)

    fa_copy.wait()
    fb_copy.wait()
    rank_row = lax.broadcasted_iota(jnp.int32, (RANK, GROUPS * RANK), 0)
    column = lax.broadcasted_iota(jnp.int32, (RANK, GROUPS * RANK), 1)
    picks = []
    for g in range(GROUPS):
        for s in range(SLOTS):
            picked = lists[g, s, d]
            picks.append((column == picked * RANK + rank_row).astype(jnp.float32))
    pick = jnp.concatenate(picks, axis=0).astype(jnp.bfloat16)
    nt = (((1,), (1,)), ((), ()))
    stage[:, 0:width] = lax.dot_general(
        pick, fav[...], nt, preferred_element_type=jnp.float32
    ).astype(jnp.bfloat16)
    stage[:, width:] = lax.dot_general(
        pick, fbv[...], nt, preferred_element_type=jnp.float32
    ).astype(jnp.bfloat16)
    block_rows = SLOTS * RANK
    mine = pl.ds(pl.multiple_of(d * block_rows, block_rows), block_rows)
    fac[mine, :] = stage[mine, :]

    def block_of(index):
        return pl.ds(pl.multiple_of(index * block_rows, block_rows), block_rows)

    for i in range(SIDE):
        group = lax.rem(partner + 2 * i, GROUPS)
        to = fac.at[mine, :] if i == 0 else relay.at[block_of(i), :]
        send(stage.at[block_of(group), :], to, dp_s, dp_r.at[0], partner, axis="dp")
    for i, peer in enumerate(along_x):
        send(stage.at[block_of(peer), :], fac.at[mine, :], dp_s, dp_r.at[1], peer, axis="dp")

    def relay_factors():
        received(relay.at[...], dp_r.at[0])
        for i, peer in enumerate(along_x):
            send(
                relay.at[block_of(i + 1), :], fac.at[block_of(partner), :],
                dp_s, dp_r.at[1], peer, axis="dp",
            )

    own.wait()

    slot_of = lax.broadcasted_iota(jnp.int32, (GROUPS * SLOTS * RANK, rows), 0) // RANK
    chosen = slot_of == entry[...].reshape(1, rows)

    def low_partial():
        received(fac.at[0 : 2 * (SIDE - 1) * block_rows], dp_r.at[1])
        everyone = lax.dot_general(
            fac[:, 0:width], xs[t], nt, preferred_element_type=jnp.float32
        )
        kept = jnp.where(chosen, everyone, 0.0)
        lrz[0] = jnp.sum(kept.reshape(GROUPS * SLOTS, RANK, rows), axis=0)
        for i in range(1, SIDE):
            send(lrz.at[0], lrz.at[i], lz_s, lz_r, at((i, 0)))

    def low_along_y():
        received(lrz.at[1:], lz_r)
        lry[0] = (lrz[0] + lrz[1]) + (lrz[2] + lrz[3])
        for i in range(1, SIDE):
            send(lry.at[0], lry.at[i], ly_s, ly_r, at((0, i)))

    def low_whole():
        received(lry.at[1:], ly_r)
        total = (lry[0] + lry[1]) + (lry[2] + lry[3])
        total = total.astype(jnp.bfloat16).astype(jnp.float32)
        spread = jnp.concatenate([total] * (GROUPS * SLOTS), axis=0)
        low[...] = jnp.transpose(jnp.where(chosen, spread, 0.0)).astype(jnp.bfloat16)
        for j in range(0, units, 256):
            columns = slice(j, min(j + 256, units))
            factors = fac[:, width + columns.start : width + columns.stop]
            extra[:, columns] = jnp.dot(low[...], factors, preferred_element_type=jnp.float32)

    def step(q, level):
        arrived(q, level)
        for o in LEVELS[q, level]:
            forward(q, o)

    def activate(p):
        some = part_rows(p)

        @pl.loop(0, panels)
        def _(j):
            columns = pl.ds(pl.multiple_of(j * 128, 128), 128)
            up_columns = pl.ds(pl.multiple_of(units + j * 128, 128), 128)
            gate = acc[some, columns] * gs[columns].reshape(1, 128)
            up = acc[some, up_columns] * us[columns].reshape(1, 128) + extra[some, columns]
            hid[some, columns] = (gate / (1.0 + jnp.exp(-gate)) * up).astype(jnp.bfloat16)

    def turn(p):
        count = PARTS[p][1]
        base = TENSOR * bases[p]
        for j in range(0, panels, 2):
            wide = min(2, panels - j)
            turned = jnp.dot(
                hid[part_rows(p), :], tv[:, j * 128 : (j + wide) * 128],
                preferred_element_type=jnp.float32,
            ).astype(jnp.bfloat16)
            for k in range(wide):
                gst[pl.ds(base + (j + k) * count, count), :] = turned[:, k * 128 : (k + 1) * 128]
        rest = TENSOR * shares[p] - panels * count
        if rest:
            gst[pl.ds(base + panels * count, rest), :] = jnp.zeros((rest, 128), jnp.bfloat16)

    def share_of(p, index):
        return pl.ds(pl.multiple_of(TENSOR * bases[p] + index * shares[p], 16), shares[p])

    def slot_of_part(p):
        return pl.ds(bases[p], shares[p])

    far_first = OFFSETS[:0:-1]

    def share_out(p):
        for o in far_first:
            peer = at(o)
            send(
                gst.at[share_of(p, peer), :], ra.at[t, slot_of_part(p), :],
                a1_s, a1_r.at[p], peer,
            )
        ra[t, slot_of_part(p), :] = gst[share_of(p, t), :]

    norm = 1.0 / math.sqrt(HIDDEN_UNITS)

    def mix(p):
        received(ra.at[1:, slot_of_part(p), :], a1_r.at[p])

        @pl.loop(0, shares[p] // 16)
        def _(k):
            tile = pl.ds(pl.multiple_of(bases[p] + k * 16, 16), 16)
            terms = [ra[i, tile, :].astype(jnp.float32) for i in range(TENSOR)]
            for bit in range(4):
                mixed = list(terms)
                for i in range(TENSOR):
                    j = i ^ (1 << bit)
                    if i < j:
                        mixed[i] = terms[i] + terms[j]
                        mixed[j] = terms[i] - terms[j]
                terms = mixed
            for i in range(TENSOR):
                rb[i, tile, :] = (terms[i] * norm).astype(jnp.bfloat16)

        for o in far_first:
            peer = at(o)
            send(
                rb.at[peer, slot_of_part(p), :], rot.at[share_of(p, t), :],
                a2_s, a2_r.at[p], peer,
            )
        rot[share_of(p, t), :] = rb[t, slot_of_part(p), :]

    def gather_back(p):
        received(rot.at[0 : (TENSOR - 1) * shares[p], :], a2_r.at[p])
        count = PARTS[p][1]
        for j in range(panels):
            rotc[part_rows(p), j * 128 : (j + 1) * 128] = rot[
                pl.ds(TENSOR * bases[p] + j * count, count), :
            ]

    def collected(q, o):
        total = part[ORDER[o], rows_of(q), :]
        for c in CHILDREN[q, o]:
            total = total + rsr[ORDER[c], rows_of(q), :].astype(jnp.float32)
        return total

    def pass_up(q, o):
        rss[ORDER[o], rows_of(q), :] = collected(q, o).astype(jnp.bfloat16)
        above = parent(q, o)
        hop = (above[0] - o[0], above[1] - o[1])
        send(
            rss.at[ORDER[o], rows_of(q), :], rsr.at[ORDER[o], rows_of(q), :],
            rs_s, rs_r.at[q, level_of(q, o)], at(hop),
        )

    def project(p):
        some = part_rows(p)
        for o in OFFSETS[::-1]:
            target = at(o, -1)
            columns = pl.ds(pl.multiple_of(target * width, width), width)
            part[ORDER[o], some, :] = jnp.dot(
                rotc[some, :], wdv[:, columns], preferred_element_type=jnp.float32
            )
            for q in TREES[p]:
                if o != (0, 0) and not CHILDREN[q, o]:
                    pass_up(q, o)

    def climb(p, level):
        for q in TREES[p]:
            received(
                rsr.at[0 : len(LEVELS[q, level + 1]), rows_of(q), :], rs_r.at[q, level + 1]
            )
            for o in LEVELS[q, level]:
                if level == 0:
                    total = collected(q, o) * ds[...].reshape(1, width)
                    out[rows_of(q), :] = total.astype(jnp.bfloat16)
                elif CHILDREN[q, o]:
                    pass_up(q, o)

    everything = pl.ds(0, rows)
    load(0, 1)
    multiply(everything, 0, 1)
    step(0, 1)
    relay_factors()
    step(2, 1)
    step(1, 1)
    step(3, 1)
    low_partial()
    load(1, 4)
    multiply(everything, 1, 4)
    step(0, 2)
    step(2, 2)
    low_along_y()
    load(5, 6)
    multiply(part_rows(0), 5, 6)
    step(1, 2)
    step(3, 2)
    table_copy.start()
    wd_copy.start()
    multiply(part_rows(1), 5, 6)
    low_whole()
    load(11, 5)
    step(0, 3)
    step(2, 3)
    multiply(part_rows(0), 11, 5)
    activate(0)
    table_copy.wait()
    turn(0)
    share_out(0)
    step(1, 3)
    step(3, 3)
    multiply(part_rows(1), 11, 5)
    activate(1)
    turn(1)
    share_out(1)
    for p in range(len(PARTS)):
        mix(p)
    wd_copy.wait()
    for p in range(len(PARTS)):
        gather_back(p)
        project(p)
    for level in (2, 1, 0):
        for p in range(len(PARTS)):
            climb(p, level)
    received(xs.at[0 : TENSOR - 1], ag_s)
    received(stage.at[...], dp_s)
    received(fac.at[0 : 2 * block_rows], dp_s)
    received(lrz.at[1:], lz_s)
    received(lry.at[1:], ly_s)
    received(ra.at[1:], a1_s)
    received(ra.at[1:], a2_s)
    received(rss.at[1:], rs_s)


def local(
    tokens,
    gate_weight_codes,
    up_weight_codes,
    down_weight_codes,
    gate_channel_scale,
    up_channel_scale,
    down_channel_scale,
    adapter_input_factors,
    adapter_output_factors,
    group_adapter_lists,
    row_adapter_entry,
):
    rows, width = tokens.shape
    units = gate_weight_codes.shape[1]
    factors = adapter_input_factors.shape[1]
    picked = GROUPS * SLOTS * RANK
    panels = units // 128
    share = sum(share_rows(count, panels) for _, count in PARTS)
    bf16, f32 = jnp.bfloat16, jnp.float32
    table = jnp.asarray(rotation_table(units), bf16)
    hbm = pl.BlockSpec(memory_space=pl.ANY)
    vmem = pl.BlockSpec(memory_space=pltpu.VMEM)
    smem = pl.BlockSpec(memory_space=pltpu.SMEM)
    dma = pltpu.SemaphoreType.DMA
    return pl.pallas_call(
        body,
        out_shape=pltpu.VMEM((rows, width), bf16),
        in_specs=[hbm, hbm, hbm, hbm, vmem, vmem, vmem, hbm, hbm, smem, vmem, hbm],
        out_specs=vmem,
        scratch_shapes=[
            pltpu.VMEM((TENSOR, rows, width), bf16),
            pltpu.VMEM((TENSOR, width, 2 * units), bf16),
            pltpu.VMEM(down_weight_codes.shape, bf16),
            pltpu.VMEM((units, units), bf16),
            pltpu.VMEM((rows, 2 * units), f32),
            pltpu.VMEM((rows, units), bf16),
            pltpu.VMEM((TENSOR * share, 128), bf16),
            pltpu.VMEM((TENSOR, share, 128), bf16),
            pltpu.VMEM((TENSOR, share, 128), bf16),
            pltpu.VMEM((TENSOR * share, 128), bf16),
            pltpu.VMEM((rows, units), bf16),
            pltpu.VMEM((TENSOR, rows, width), f32),
            pltpu.VMEM((TENSOR, rows, width), bf16),
            pltpu.VMEM((TENSOR, rows, width), bf16),
            pltpu.VMEM((width, factors), bf16),
            pltpu.VMEM((units, factors), bf16),
            pltpu.VMEM((picked, width + units), bf16),
            pltpu.VMEM((picked, width + units), bf16),
            pltpu.VMEM((SIDE * SLOTS * RANK, width + units), bf16),
            pltpu.VMEM((SIDE, RANK, rows), f32),
            pltpu.VMEM((SIDE, RANK, rows), f32),
            pltpu.VMEM((rows, picked), bf16),
            pltpu.VMEM((rows, units), f32),
            dma,
            dma((TENSOR,)),
            dma((4,)),
            dma,
            dma((QUARTERS, SIDE)),
            dma,
            dma((2,)),
            dma,
            dma,
            dma,
            dma,
            dma,
            dma((len(PARTS),)),
            dma,
            dma((len(PARTS),)),
            dma,
            dma((QUARTERS, SIDE)),
        ],
        compiler_params=pltpu.CompilerParams(
            collective_id=0, has_side_effects=True, vmem_limit_bytes=60 * MIB
        ),
    )(
        tokens,
        gate_weight_codes,
        up_weight_codes,
        down_weight_codes,
        gate_channel_scale,
        up_channel_scale,
        down_channel_scale,
        adapter_input_factors,
        adapter_output_factors,
        jnp.transpose(group_adapter_lists, (0, 2, 1)),
        row_adapter_entry,
        table,
    )


def solution(mesh):
    return jax.shard_map(
        local,
        mesh=mesh,
        in_specs=(
            P("dp", "tensor"),
            P(None, "tensor"),
            P(None, "tensor"),
            P("tensor", None),
            P("tensor"),
            P("tensor"),
            P("tensor"),
            P(None, "dp"),
            P("tensor", "dp"),
            P(),
            P("dp"),
        ),
        out_specs=P("dp", "tensor"),
        check_vma=False,
    )
```

time: 86.7 us -> 72.6 us (0.84)
  Pallas kernels: 84.9 us -> 71.8 us
  local copies, waits for them, and re-layouts: 1.62 us -> 0.68 us
    pallas_call x1, Pallas kernels: 84.9 us -> 71.8 us  [local(): pl.pallas_call(body, out_shape=pltpu.VMEM((rows, width), bf16), in_specs=...]
    unnamed x1, local copies, waits for them, and re-layouts: 1.62 us -> 0.68 us
where the time goes in v3:
time: 72.6 us; the launch traced here: 72.5 us
  Pallas kernels  71.8 us (99%)
    pallas_call x1, Pallas kernels, local(): pl.pallas_call(body, out_shape=pltpu.VMEM((rows, width), bf16), in_specs=...  71.8 us

profile of v3, /device:TPU:0, one launch (start us, length us, event | category | flops | bytes accessed | tf_op | source)
XLA Modules:
  0.0 72.5 jit_solution(5809878398872989750)
XLA Ops:
  0.0 71.8 %shard_map.118 = bf16[384,256]{1,0:T(8,128)(2,1)S(1)} custom-call(bf16[384,256]{1,0:T(8,128)(2,1)} %tokens.1, bf16[4096,896]{1,0:T(8,128)(2,1)} %wg.1, bf16[4096,896]{1,0:T(8,128)(2,1)} %wu.1, bf16[896,4096]{1,0:T(8,128)(2,1)} %wd.1, f32[896]{0:T(1024)} %gs.1, f32[896]{0:T(1024)} %us.1, f32[256]{0:T(256)} %ds.1, bf16[4096,128]{1,0:T(8,128)(2,1)} %fa.1, ...), custom_call_target="tpu_custom_call" | custom-call | tf_op jit(solution)/shard_map/pallas_call | solution.py:470
  71.8 0.7 copy.14

commit v4 on v3

--- a/solution.py
+++ b/solution.py
@@ -88,7 +88,7 @@
 def body(
     tokens, wg, wu, wd, gs, us, ds, fa, fb, lists, entry, table, out,
     xs, wv, wdv, tv, acc, hid, gst, ra, rb, rot, rotc, part, rss, rsr,
-    fav, fbv, stage, fac, relay, lrz, lry, low, extra,
+    fav, fbv, stage, fac, lrz, lry, low, extra,
     own_sem, w_sem, misc_sem, ag_s, ag_r, dp_s, dp_r, lz_s, lz_r, ly_s, ly_r,
     a1_s, a1_r, a2_s, a2_r, rs_s, rs_r,
 ):
@@ -124,10 +124,8 @@
         pl.semaphore_signal(
             barrier, inc=1, device_id={"tensor": at(o)}, device_id_type=pl.DeviceIdType.MESH
         )
-    core = lax.rem(d, 2)
-    partner = d + 1 - 2 * core
-    along_x = [lax.rem(d + 2 * i, GROUPS) for i in range(1, SIDE)]
-    for peer in [partner] + along_x:
+    others = [lax.rem(d + i, GROUPS) for i in range(1, GROUPS)]
+    for peer in others:
         pl.semaphore_signal(
             barrier, inc=1, device_id={"dp": peer}, device_id_type=pl.DeviceIdType.MESH
         )
@@ -151,47 +149,6 @@
     fetch(0, 5)
     table_copy = pltpu.make_async_copy(table, tv, misc_sem.at[2])
     wd_copy = pltpu.make_async_copy(wd, wdv, misc_sem.at[3])
-
-    pl.semaphore_wait(barrier, len(NEAR) + len(OPPOSITE) + SIDE)
-
-    def rows_of(q):
-        return pl.ds(*TREE_ROWS[q])
-
-    def part_rows(p):
-        return pl.ds(*PARTS[p])
-
-    def forward(q, o):
-        source = at(o, -1)
-        for c in CHILDREN[q, o]:
-            hop = (c[0] - o[0], c[1] - o[1])
-            src = tokens.at[rows_of(q), :] if o == (0, 0) else xs.at[source, rows_of(q), :]
-            send(
-                src, xs.at[source, rows_of(q), :],
-                ag_s, ag_r.at[q, level_of(q, c)], at(hop),
-            )
-
-    def arrived(q, level):
-        received(xs.at[0 : len(LEVELS[q, level]), rows_of(q), :], ag_r.at[q, level])
-
-    def load(first, count):
-        for i in range(first, first + count):
-            received(wv.at[i], w_sem.at[i])
-
-    def multiply(some, first, count):
-        sources = [at(OFFSETS[i], -1) for i in range(first, first + count)]
-        for n in range(2 * units // 256):
-            columns = slice(n * 256, (n + 1) * 256)
-            x = jnp.concatenate([xs[source, some, :] for source in sources], axis=1)
-            w = wv[first : first + count, :, columns].reshape(count * width, 256)
-            product = jnp.dot(x, w, preferred_element_type=jnp.float32)
-            if first == 0:
-                acc[some, columns] = product
-            else:
-                acc[some, columns] += product
-
-    for q in TREE_ROWS:
-        forward(q, (0, 0))
-    fetch(5, 11)
 
     fa_copy.wait()
     fb_copy.wait()
@@ -214,23 +171,59 @@
     mine = pl.ds(pl.multiple_of(d * block_rows, block_rows), block_rows)
     fac[mine, :] = stage[mine, :]
 
+    pl.semaphore_wait(barrier, len(NEAR) + len(OPPOSITE) + GROUPS - 1)
+
+    def rows_of(q):
+        return pl.ds(*TREE_ROWS[q])
+
+    def part_rows(p):
+        return pl.ds(*PARTS[p])
+
+    def forward(q, o):
+        source = at(o, -1)
+        for c in CHILDREN[q, o]:
+            hop = (c[0] - o[0], c[1] - o[1])
+            src = tokens.at[rows_of(q), :] if o == (0, 0) else xs.at[source, rows_of(q), :]
+            send(
+                src, xs.at[source, rows_of(q), :],
+                ag_s, ag_r.at[q, level_of(q, c)], at(hop),
+            )
+
+    def arrived(q, level):
+        received(xs.at[0 : len(LEVELS[q, level]), rows_of(q), :], ag_r.at[q, level])
+
+    def load(first, count):
+        for i in range(first, first + count):
+            received(wv.at[i], w_sem.at[i])
+
+    def multiply(some, first, count):
+        sources = [at(OFFSETS[i], -1) for i in range(first, first + count)]
+        for n in range(2 * units // 256):
+            columns = slice(n * 256, (n + 1) * 256)
+            x = jnp.concatenate([xs[source, some, :] for source in sources], axis=1)
+            w = wv[first : first + count, :, columns].reshape(count * width, 256)
+            product = jnp.dot(x, w, preferred_element_type=jnp.float32)
+            if first == 0:
+                acc[some, columns] = product
+            else:
+                acc[some, columns] += product
+
     def block_of(index):
         return pl.ds(pl.multiple_of(index * block_rows, block_rows), block_rows)
 
-    for i in range(SIDE):
-        group = lax.rem(partner + 2 * i, GROUPS)
-        to = fac.at[mine, :] if i == 0 else relay.at[block_of(i), :]
-        send(stage.at[block_of(group), :], to, dp_s, dp_r.at[0], partner, axis="dp")
-    for i, peer in enumerate(along_x):
-        send(stage.at[block_of(peer), :], fac.at[mine, :], dp_s, dp_r.at[1], peer, axis="dp")
-
-    def relay_factors():
-        received(relay.at[...], dp_r.at[0])
-        for i, peer in enumerate(along_x):
-            send(
-                relay.at[block_of(i + 1), :], fac.at[block_of(partner), :],
-                dp_s, dp_r.at[1], peer, axis="dp",
-            )
+    into, out_of = slice(0, width), slice(width, width + units)
+    for peer in others:
+        send(
+            stage.at[block_of(peer), into], fac.at[mine, into], dp_s, dp_r.at[0], peer, axis="dp"
+        )
+    for q in TREE_ROWS:
+        forward(q, (0, 0))
+    for peer in others:
+        send(
+            stage.at[block_of(peer), out_of], fac.at[mine, out_of],
+            dp_s, dp_r.at[1], peer, axis="dp",
+        )
+    fetch(5, 11)
 
     own.wait()
 
@@ -238,7 +231,7 @@
     chosen = slot_of == entry[...].reshape(1, rows)
 
     def low_partial():
-        received(fac.at[0 : 2 * (SIDE - 1) * block_rows], dp_r.at[1])
+        received(fac.at[0 : (GROUPS - 1) * block_rows, into], dp_r.at[0])
         everyone = lax.dot_general(
             fac[:, 0:width], xs[t], nt, preferred_element_type=jnp.float32
         )
@@ -255,6 +248,7 @@
 
     def low_whole():
         received(lry.at[1:], ly_r)
+        received(fac.at[0 : (GROUPS - 1) * block_rows, out_of], dp_r.at[1])
         total = (lry[0] + lry[1]) + (lry[2] + lry[3])
         total = total.astype(jnp.bfloat16).astype(jnp.float32)
         spread = jnp.concatenate([total] * (GROUPS * SLOTS), axis=0)
@@ -363,9 +357,9 @@
             rs_s, rs_r.at[q, level_of(q, o)], at(hop),
         )
 
-    def project(p):
+    def project(p, offsets):
         some = part_rows(p)
-        for o in OFFSETS[::-1]:
+        for o in offsets:
             target = at(o, -1)
             columns = pl.ds(pl.multiple_of(target * width, width), width)
             part[ORDER[o], some, :] = jnp.dot(
@@ -390,25 +384,24 @@
     everything = pl.ds(0, rows)
     load(0, 1)
     multiply(everything, 0, 1)
+    low_partial()
     step(0, 1)
-    relay_factors()
     step(2, 1)
+    low_along_y()
     step(1, 1)
     step(3, 1)
-    low_partial()
     load(1, 4)
     multiply(everything, 1, 4)
     step(0, 2)
     step(2, 2)
-    low_along_y()
+    step(1, 2)
+    step(3, 2)
     load(5, 6)
     multiply(part_rows(0), 5, 6)
-    step(1, 2)
-    step(3, 2)
+    low_whole()
     table_copy.start()
     wd_copy.start()
     multiply(part_rows(1), 5, 6)
-    low_whole()
     load(11, 5)
     step(0, 3)
     step(2, 3)
@@ -426,15 +419,15 @@
     for p in range(len(PARTS)):
         mix(p)
     wd_copy.wait()
-    for p in range(len(PARTS)):
-        gather_back(p)
-        project(p)
+    gather_back(0)
+    project(0, OFFSETS[::-1])
+    gather_back(1)
+    project(1, OFFSETS[::-1])
     for level in (2, 1, 0):
         for p in range(len(PARTS)):
             climb(p, level)
     received(xs.at[0 : TENSOR - 1], ag_s)
-    received(stage.at[...], dp_s)
-    received(fac.at[0 : 2 * block_rows], dp_s)
+    received(fac.at[0 : (GROUPS - 1) * block_rows], dp_s)
     received(lrz.at[1:], lz_s)
     received(lry.at[1:], ly_s)
     received(ra.at[1:], a1_s)
@@ -491,7 +484,6 @@
             pltpu.VMEM((units, factors), bf16),
             pltpu.VMEM((picked, width + units), bf16),
             pltpu.VMEM((picked, width + units), bf16),
-            pltpu.VMEM((SIDE * SLOTS * RANK, width + units), bf16),
             pltpu.VMEM((SIDE, RANK, rows), f32),
             pltpu.VMEM((SIDE, RANK, rows), f32),
             pltpu.VMEM((rows, picked), bf16),

time: 72.6 us -> 70.4 us (0.970)
  Pallas kernels: 71.8 us -> 69.6 us
    pallas_call x1, Pallas kernels: 71.8 us -> 69.6 us  [local(): pl.pallas_call(body, out_shape=pltpu.VMEM((rows, width), bf16), in_specs=...]
where the time goes in v4:
time: 70.4 us; the launch traced here: 70.2 us
  Pallas kernels  69.6 us (99%)
    pallas_call x1, Pallas kernels, local(): pl.pallas_call(body, out_shape=pltpu.VMEM((rows, width), bf16), in_specs=...  69.6 us

profile of v4, /device:TPU:0, one launch (start us, length us, event | category | flops | bytes accessed | tf_op | source)
XLA Modules:
  0.0 70.2 jit_solution(3644184828619859052)
XLA Ops:
  0.0 69.6 %shard_map.118 = bf16[384,256]{1,0:T(8,128)(2,1)S(1)} custom-call(bf16[384,256]{1,0:T(8,128)(2,1)} %tokens.1, bf16[4096,896]{1,0:T(8,128)(2,1)} %wg.1, bf16[4096,896]{1,0:T(8,128)(2,1)} %wu.1, bf16[896,4096]{1,0:T(8,128)(2,1)} %wd.1, f32[896]{0:T(1024)} %gs.1, f32[896]{0:T(1024)} %us.1, f32[256]{0:T(256)} %ds.1, bf16[4096,128]{1,0:T(8,128)(2,1)} %fa.1, ...), custom_call_target="tpu_custom_call" | custom-call | tf_op jit(solution)/shard_map/pallas_call | solution.py:463
  69.6 0.7 copy.14

commit v5 on v4

--- a/solution.py
+++ b/solution.py
@@ -19,6 +19,7 @@
 PARTS = ((0, 208), (208, 176))
 TREES = ((0, 2), (1, 3))
 TREE_ROWS = {0: (0, 96), 2: (96, 112), 1: (208, 96), 3: (304, 80)}
+GROUPS_OF_BLOCKS = ((0, 1), (1, 4), (5, 6), (11, 5))
 MIB = 1024 * 1024
 
 
@@ -86,9 +87,9 @@
 
 
 def body(
-    tokens, wg, wu, wd, gs, us, ds, fa, fb, lists, entry, table, out,
+    tokens, wg, wu, wd, gs_in, us_in, ds_in, fa, fb, lists_in, entry_in, table, out,
     xs, wv, wdv, tv, acc, hid, gst, ra, rb, rot, rotc, part, rss, rsr,
-    fav, fbv, stage, fac, lrz, lry, low, extra,
+    fav, fbv, stage, fac, lrz, lry, low, extra, gs, us, ds, lists, entry,
     own_sem, w_sem, misc_sem, ag_s, ag_r, dp_s, dp_r, lz_s, lz_r, ly_s, ly_r,
     a1_s, a1_r, a2_s, a2_r, rs_s, rs_r,
 ):
@@ -130,6 +131,13 @@
             barrier, inc=1, device_id={"dp": peer}, device_id_type=pl.DeviceIdType.MESH
         )
 
+    small = [
+        pltpu.make_async_copy(src, dst, misc_sem.at[4 + i])
+        for i, (src, dst) in enumerate(
+            ((lists_in, lists), (entry_in, entry), (gs_in, gs), (us_in, us), (ds_in, ds))
+        )
+    ]
+    small[0].start()
     own = pltpu.make_async_copy(tokens, xs.at[t], own_sem)
     own.start()
     fa_copy = pltpu.make_async_copy(
@@ -138,18 +146,23 @@
     fa_copy.start()
     fb_copy = pltpu.make_async_copy(fb, fbv, misc_sem.at[1])
     fb_copy.start()
-    def fetch(first, count):
+    for copy in small[1:]:
+        copy.start()
+    def fetch(group):
+        first, count = GROUPS_OF_BLOCKS[group]
         for i in range(first, first + count):
             block = pl.ds(pl.multiple_of(at(OFFSETS[i], -1) * width, width), width)
-            pltpu.make_async_copy(wg.at[block, :], wv.at[i, :, 0:units], w_sem.at[i]).start()
+            pltpu.make_async_copy(wg.at[block, :], wv.at[i, :, 0:units], w_sem.at[group]).start()
             pltpu.make_async_copy(
-                wu.at[block, :], wv.at[i, :, units : 2 * units], w_sem.at[i]
+                wu.at[block, :], wv.at[i, :, units : 2 * units], w_sem.at[group]
             ).start()
 
-    fetch(0, 5)
+    fetch(0)
+    fetch(1)
     table_copy = pltpu.make_async_copy(table, tv, misc_sem.at[2])
     wd_copy = pltpu.make_async_copy(wd, wdv, misc_sem.at[3])
 
+    small[0].wait()
     fa_copy.wait()
     fb_copy.wait()
     rank_row = lax.broadcasted_iota(jnp.int32, (RANK, GROUPS * RANK), 0)
@@ -192,9 +205,9 @@
     def arrived(q, level):
         received(xs.at[0 : len(LEVELS[q, level]), rows_of(q), :], ag_r.at[q, level])
 
-    def load(first, count):
-        for i in range(first, first + count):
-            received(wv.at[i], w_sem.at[i])
+    def load(group):
+        first, count = GROUPS_OF_BLOCKS[group]
+        received(wv.at[first : first + count], w_sem.at[group])
 
     def multiply(some, first, count):
         sources = [at(OFFSETS[i], -1) for i in range(first, first + count)]
@@ -223,9 +236,12 @@
             stage.at[block_of(peer), out_of], fac.at[mine, out_of],
             dp_s, dp_r.at[1], peer, axis="dp",
         )
-    fetch(5, 11)
+    fetch(2)
+    fetch(3)
 
     own.wait()
+    for copy in small[1:]:
+        copy.wait()
 
     slot_of = lax.broadcasted_iota(jnp.int32, (GROUPS * SLOTS * RANK, rows), 0) // RANK
     chosen = slot_of == entry[...].reshape(1, rows)
@@ -382,7 +398,7 @@
                     pass_up(q, o)
 
     everything = pl.ds(0, rows)
-    load(0, 1)
+    load(0)
     multiply(everything, 0, 1)
     low_partial()
     step(0, 1)
@@ -390,19 +406,19 @@
     low_along_y()
     step(1, 1)
     step(3, 1)
-    load(1, 4)
+    load(1)
     multiply(everything, 1, 4)
     step(0, 2)
     step(2, 2)
     step(1, 2)
     step(3, 2)
-    load(5, 6)
+    load(2)
     multiply(part_rows(0), 5, 6)
     low_whole()
     table_copy.start()
     wd_copy.start()
     multiply(part_rows(1), 5, 6)
-    load(11, 5)
+    load(3)
     step(0, 3)
     step(2, 3)
     multiply(part_rows(0), 11, 5)
@@ -458,12 +474,11 @@
     table = jnp.asarray(rotation_table(units), bf16)
     hbm = pl.BlockSpec(memory_space=pl.ANY)
     vmem = pl.BlockSpec(memory_space=pltpu.VMEM)
-    smem = pl.BlockSpec(memory_space=pltpu.SMEM)
     dma = pltpu.SemaphoreType.DMA
     return pl.pallas_call(
         body,
         out_shape=pltpu.VMEM((rows, width), bf16),
-        in_specs=[hbm, hbm, hbm, hbm, vmem, vmem, vmem, hbm, hbm, smem, vmem, hbm],
+        in_specs=[hbm] * 12,
         out_specs=vmem,
         scratch_shapes=[
             pltpu.VMEM((TENSOR, rows, width), bf16),
@@ -488,9 +503,14 @@
             pltpu.VMEM((SIDE, RANK, rows), f32),
             pltpu.VMEM((rows, picked), bf16),
             pltpu.VMEM((rows, units), f32),
-            dma,
-            dma((TENSOR,)),
-            dma((4,)),
+            pltpu.VMEM(gate_channel_scale.shape, f32),
+            pltpu.VMEM(up_channel_scale.shape, f32),
+            pltpu.VMEM(down_channel_scale.shape, f32),
+            pltpu.SMEM((GROUPS, SLOTS, GROUPS), jnp.int32),
+            pltpu.VMEM(row_adapter_entry.shape, jnp.int32),
+            dma,
+            dma((len(GROUPS_OF_BLOCKS),)),
+            dma((9,)),
             dma,
             dma((QUARTERS, SIDE)),
             dma,

time: 70.4 us -> 69.3 us (0.984)
  Pallas kernels: 69.6 us -> 68.6 us
    pallas_call x1, Pallas kernels: 69.6 us -> 68.6 us  [local(): pl.pallas_call(body, out_shape=pltpu.VMEM((rows, width), bf16), in_specs=...]
where the time goes in v5:
time: 69.3 us; the launch traced here: 69.2 us
  Pallas kernels  68.6 us (99%)
    pallas_call x1, Pallas kernels, local(): pl.pallas_call(body, out_shape=pltpu.VMEM((rows, width), bf16), in_specs=...  68.6 us

profile of v5, /device:TPU:0, one launch (start us, length us, event | category | flops | bytes accessed | tf_op | source)
XLA Modules:
  0.0 69.2 jit_solution(12336925713141148518)
XLA Ops:
  0.0 68.6 %shard_map.118 = bf16[384,256]{1,0:T(8,128)(2,1)S(1)} custom-call(bf16[384,256]{1,0:T(8,128)(2,1)} %tokens.1, bf16[4096,896]{1,0:T(8,128)(2,1)} %wg.1, bf16[4096,896]{1,0:T(8,128)(2,1)} %wu.1, bf16[896,4096]{1,0:T(8,128)(2,1)} %wd.1, f32[896]{0:T(1024)} %gs_in.1, f32[896]{0:T(1024)} %us_in.1, f32[256]{0:T(256)} %ds_in.1, bf16[4096,128]{1,0:T(8,128)(2,1)} %fa.1, ...), custom_call_target="tpu_custom_call" | custom-call | tf_op jit(solution)/shard_map/pallas_call | solution.py:478
  68.6 0.7 copy.14

commit v6 on v5

--- a/solution.py
+++ b/solution.py
@@ -209,14 +209,14 @@
         first, count = GROUPS_OF_BLOCKS[group]
         received(wv.at[first : first + count], w_sem.at[group])
 
-    def multiply(some, first, count):
-        sources = [at(OFFSETS[i], -1) for i in range(first, first + count)]
+    def multiply(some, blocks):
+        sources = [at(OFFSETS[i], -1) for i in blocks]
         for n in range(2 * units // 256):
             columns = slice(n * 256, (n + 1) * 256)
             x = jnp.concatenate([xs[source, some, :] for source in sources], axis=1)
-            w = wv[first : first + count, :, columns].reshape(count * width, 256)
+            w = jnp.concatenate([wv[i, :, columns] for i in blocks], axis=0)
             product = jnp.dot(x, w, preferred_element_type=jnp.float32)
-            if first == 0:
+            if 0 in blocks:
                 acc[some, columns] = product
             else:
                 acc[some, columns] += product
@@ -278,6 +278,13 @@
         arrived(q, level)
         for o in LEVELS[q, level]:
             forward(q, o)
+
+    def last_blocks(p, level):
+        for q in TREES[p]:
+            multiply(
+                rows_of(q),
+                [ORDER[o] for o in LEVELS[q, level] if ORDER[o] >= GROUPS_OF_BLOCKS[-1][0]],
+            )
 
     def activate(p):
         some = part_rows(p)
@@ -399,7 +406,7 @@
 
     everything = pl.ds(0, rows)
     load(0)
-    multiply(everything, 0, 1)
+    multiply(everything, range(0, 1))
     low_partial()
     step(0, 1)
     step(2, 1)
@@ -407,28 +414,30 @@
     step(1, 1)
     step(3, 1)
     load(1)
-    multiply(everything, 1, 4)
+    multiply(everything, range(1, 5))
     step(0, 2)
     step(2, 2)
     step(1, 2)
     step(3, 2)
     load(2)
-    multiply(part_rows(0), 5, 6)
+    multiply(part_rows(0), range(5, 11))
     low_whole()
     table_copy.start()
     wd_copy.start()
-    multiply(part_rows(1), 5, 6)
+    multiply(part_rows(1), range(5, 11))
     load(3)
+    last_blocks(0, 2)
     step(0, 3)
     step(2, 3)
-    multiply(part_rows(0), 11, 5)
+    last_blocks(0, 3)
     activate(0)
     table_copy.wait()
     turn(0)
     share_out(0)
+    last_blocks(1, 2)
     step(1, 3)
     step(3, 3)
-    multiply(part_rows(1), 11, 5)
+    last_blocks(1, 3)
     activate(1)
     turn(1)
     share_out(1)

time: 69.3 us -> 70.9 us (1.023)
  Pallas kernels: 68.6 us -> 70.1 us
    pallas_call x1, Pallas kernels: 68.6 us -> 70.1 us  [local(): pl.pallas_call(body, out_shape=pltpu.VMEM((rows, width), bf16), in_specs=...]
where the time goes in v6:
time: 70.9 us; the launch traced here: 70.8 us
  Pallas kernels  70.1 us (99%)
    pallas_call x1, Pallas kernels, local(): pl.pallas_call(body, out_shape=pltpu.VMEM((rows, width), bf16), in_specs=...  70.1 us

profile of v6, /device:TPU:0, one launch (start us, length us, event | category | flops | bytes accessed | tf_op | source)
XLA Modules:
  0.0 70.8 jit_solution(10078274600232466631)
XLA Ops:
  0.0 70.1 %shard_map.118 = bf16[384,256]{1,0:T(8,128)(2,1)S(1)} custom-call(bf16[384,256]{1,0:T(8,128)(2,1)} %tokens.1, bf16[4096,896]{1,0:T(8,128)(2,1)} %wg.1, bf16[4096,896]{1,0:T(8,128)(2,1)} %wu.1, bf16[896,4096]{1,0:T(8,128)(2,1)} %wd.1, f32[896]{0:T(1024)} %gs_in.1, f32[896]{0:T(1024)} %us_in.1, f32[256]{0:T(256)} %ds_in.1, bf16[4096,128]{1,0:T(8,128)(2,1)} %fa.1, ...), custom_call_target="tpu_custom_call" | custom-call | tf_op jit(solution)/shard_map/pallas_call | solution.py:487
  70.2 0.7 copy.14
